TPU v7x, 32 devices: a whole 2x2x4 slice. The times are simulated.
32 devices in a mesh: group: 2 (over x), frame: 16 (over z, y, core).
Axes of the slice: x: 2, y: 2, z: 4, core: 2. Of those that a mesh axis runs over, the one named last changes fastest.
Arguments:
- queries: bfloat16 [10240, 5120], P(('group', 'frame')), parts along dimension 0, may hold values from -33 to 33
- keys: bfloat16 [10240, 5120], P(('group', 'frame')), parts along dimension 0, may hold values from -33 to 33
- values: bfloat16 [10240, 5120], P(('group', 'frame')), parts along dimension 0, may hold values from -6 to 6
- labels: int32 [80], P('group'), parts along dimension 0, may hold values from 0 to 1, as said below
- band: int32 [80], P('group'), parts along dimension 0, may hold values from 2 to 4
Outputs:
- attended: bfloat16 [10240, 5120], P(('group', 'frame')), parts along dimension 0
There are 2 independent parts, one for each index of `group`. A program takes and returns all parts, laid end to end along the dimension named above; each array names one. Nothing has to cross between parts.
Inputs may be any that keep to these rules, and one draw needn't show every extreme that they name: `labels`: exactly 10 of the 40 heads carry 1, the others 0.
All inputs are finite; a program needn't handle non-finite values.
Results may differ from a plain program's by a relative error of at most 0.0049.
Values may be sent and summed in bfloat16 or wider, within the bound.
No kernel may reach another device: no remote copies, remote signals or barrier semaphores. Data moves between devices by JAX's collectives and lax.ppermute only.
A program may use at most 128 MiB of HBM per device.

v0:
```python
import functools
import math

import jax
import jax.numpy as jnp
from jax import lax
from jax.experimental import pallas as pl
from jax.experimental.pallas import tpu as pltpu
from jax.sharding import PartitionSpec as P

TEMP_HEADS = 10
HEAD_DIM = 128
PIXEL_BLOCK = 32
SPATIAL_PIECES = (9, 6, 15)
STEP_HEADS = 3
HIGH = 5
LEVELS = (0, 2, 3, 4, 5, 6, 2 * (TEMP_HEADS - HIGH))
MASKED = -1e30
MIB = 1024 * 1024
HBM = pl.BlockSpec(memory_space=pltpu.HBM)
SMEM = pl.BlockSpec(memory_space=pltpu.SMEM)
VMEM = pl.BlockSpec(memory_space=pltpu.VMEM)


def swap_bit(block, bit):
    count = lax.axis_size("frame")
    return lax.ppermute(block, "frame", [(i, i ^ (1 << bit)) for i in range(count)])


def swap_pairs(block, first, distance):
    count = lax.axis_size("frame")
    places = count // 4
    route = []
    for low in range(first, places - 1, 2):
        if low - (distance - 1) >= 0:
            route += [(low * 4 + i, low * 4 + 4 + i) for i in range(4)]
        if low + distance < places:
            route += [(low * 4 + 4 + i, low * 4 + i) for i in range(4)]
    return lax.ppermute(block, "frame", route)


def largest(value):
    count = lax.axis_size("group")
    result = value
    for shift in range(1, count):
        route = [(i, (i + shift) % count) for i in range(count)]
        result = jnp.maximum(result, lax.ppermute(value, "group", route))
    return result


def position():
    index = lax.axis_index("frame")
    return (index // 2) % 2, index // 4


def columns_of(head):
    return pl.ds(pl.multiple_of(head * HEAD_DIM, HEAD_DIM), HEAD_DIM)


def rows_of(side, half):
    return pl.ds(pl.multiple_of(side * half, half), half)


def extract_kernel(
    reach, labels_hbm, band_hbm, keys, values,
    meta, choice, pair_keep, high_send, low_send, labels, band, found, sems,
):
    heads = labels.shape[0]
    half = pair_keep.shape[2]
    side, _ = position()
    small = [
        pltpu.make_async_copy(labels_hbm, labels, sems.at[0]),
        pltpu.make_async_copy(band_hbm, band, sems.at[1]),
    ]
    for copy in small:
        copy.start()
    for copy in small:
        copy.wait()

    temporal = jnp.int32(0)
    for head in range(heads):
        found[temporal] = head
        temporal = temporal + labels[head]
    listed_heads = [found[number] for number in range(TEMP_HEADS)]
    bands = [band[head] for head in listed_heads]
    kept, sent = rows_of(side, half), rows_of(1 - side, half)
    for number, head in enumerate(listed_heads):
        rank = jnp.int32(0)
        for other in range(TEMP_HEADS):
            if other != number:
                before = bands[other] >= bands[number] if other < number else bands[other] > bands[number]
                rank = rank + before.astype(jnp.int32)
        meta[heads + rank] = head
        meta[2 * heads + rank] = bands[number]
        columns = columns_of(head)
        for kind, source in enumerate((keys, values)):
            pltpu.make_async_copy(source.at[kept, columns], pair_keep.at[rank, kind], sems.at[2]).start()

            @pl.when(rank < HIGH)
            def _():
                pltpu.make_async_copy(source.at[sent, columns], high_send.at[rank, kind], sems.at[3]).start()

            @pl.when(rank >= HIGH)
            def _():
                pltpu.make_async_copy(source.at[sent, columns], low_send.at[rank - HIGH, kind], sems.at[4]).start()

    spatial = jnp.int32(0)
    for head in range(heads):
        meta[spatial] = head
        spatial = jnp.minimum(spatial + 1 - labels[head], heads - TEMP_HEADS)
    items = 3 * heads
    places = items + 2 * TEMP_HEADS
    for number in range(2 * TEMP_HEADS):
        meta[items + number] = 0
    listed = jnp.int32(0)
    for number in range(TEMP_HEADS - HIGH):
        for kind in range(2):
            is_needed = meta[2 * heads + HIGH + number] >= 2 * reach - 1 + kind
            meta[places + 2 * number + kind] = listed

            @pl.when(is_needed)
            def _():
                meta[items + listed] = 2 * number + kind

            listed = listed + is_needed.astype(jnp.int32)
    choice[0] = sum((listed > level).astype(jnp.int32) for level in LEVELS[:-1])
    for number, whole in enumerate((pair_keep, high_send, low_send)):
        pltpu.make_async_copy(whole, whole, sems.at[2 + number]).wait()


def extract(reach, labels, band, keys, values):
    half = keys.shape[0] // 2
    pair = [
        jax.ShapeDtypeStruct((count, 2, half, HEAD_DIM), jnp.bfloat16)
        for count in (TEMP_HEADS, HIGH, TEMP_HEADS - HIGH)
    ]
    return pl.pallas_call(
        functools.partial(extract_kernel, reach),
        out_shape=(
            jax.ShapeDtypeStruct((3 * labels.shape[0] + 4 * TEMP_HEADS,), jnp.int32),
            jax.ShapeDtypeStruct((1,), jnp.int32),
            *pair,
        ),
        in_specs=[HBM] * 4,
        out_specs=(SMEM, SMEM) + (VMEM,) * 3,
        scratch_shapes=[
            pltpu.SMEM(labels.shape, jnp.int32),
            pltpu.SMEM(band.shape, jnp.int32),
            pltpu.SMEM((TEMP_HEADS + 1,), jnp.int32),
            pltpu.SemaphoreType.DMA((5,)),
        ],
        compiler_params=pltpu.CompilerParams(vmem_limit_bytes=58 * MIB),
        cost_estimate=pl.CostEstimate(flops=0, bytes_accessed=8 * TEMP_HEADS * half * HEAD_DIM * 2, transcendentals=0),
        name="extract_temporal",
    )(labels, band, keys, values)


def queries_kernel(meta, queries, query_keep, query_send, sems):
    heads = (meta.shape[0] - 4 * TEMP_HEADS) // 3
    half = query_keep.shape[1]
    side, _ = position()
    kept, sent = rows_of(side, half), rows_of(1 - side, half)
    for number in range(TEMP_HEADS):
        columns = columns_of(meta[heads + number])
        pltpu.make_async_copy(queries.at[kept, columns], query_keep.at[number], sems.at[0]).start()
        pltpu.make_async_copy(queries.at[sent, columns], query_send.at[number], sems.at[1]).start()
    for number, whole in enumerate((query_keep, query_send)):
        pltpu.make_async_copy(whole, whole, sems.at[number]).wait()


def extract_queries(meta, queries):
    half = queries.shape[0] // 2
    single = jax.ShapeDtypeStruct((TEMP_HEADS, half, HEAD_DIM), jnp.bfloat16)
    return pl.pallas_call(
        queries_kernel,
        out_shape=(single, single),
        in_specs=[SMEM, HBM],
        out_specs=(VMEM, VMEM),
        scratch_shapes=[pltpu.SemaphoreType.DMA((2,))],
        compiler_params=pltpu.CompilerParams(vmem_limit_bytes=50 * MIB),
        cost_estimate=pl.CostEstimate(flops=0, bytes_accessed=4 * TEMP_HEADS * half * HEAD_DIM * 2, transcendentals=0),
        name="extract_queries",
    )(meta, queries)


def spatial_kernel(scale, first, meta, *refs):
    heads = [refs[5 * number : 5 * number + 5] for number in range(STEP_HEADS)]
    out, held, sems = refs[-3:]
    step, steps = pl.program_id(0), pl.num_programs(0)
    slot = step % 2
    rows = held.shape[2]
    half = rows // 2

    def store(step, slot, number):
        columns = columns_of(meta[first + step * STEP_HEADS + number])
        return pltpu.make_async_copy(held.at[slot, number], out.at[:, columns], sems.at[slot, number])

    @pl.when(step >= 2)
    def _():
        for number in range(STEP_HEADS):
            store(step - 2, slot, number).wait()

    key = [jnp.concatenate([key_own[...], key_far[...]], axis=0) for _, key_own, _, key_far, _ in heads]
    value = [jnp.concatenate([value_own[...], value_far[...]], axis=0) for _, _, value_own, _, value_far in heads]
    parts = [(number, slice(start, start + half)) for number in range(STEP_HEADS) for start in (0, half)]
    scores = [
        lax.dot_general(
            heads[number][0][part, :], key[number], (((1,), (1,)), ((), ())), preferred_element_type=jnp.float32
        )
        for number, part in parts
    ]
    for (number, part), score in zip(parts, scores):
        peak = jnp.max(score, axis=1, keepdims=True)
        weights = jnp.exp2((score - peak) * scale)
        total = jnp.sum(weights, axis=1, keepdims=True)
        result = jnp.dot(weights.astype(jnp.bfloat16), value[number], preferred_element_type=jnp.float32)
        held[slot, number, part, :] = (result / total).astype(jnp.bfloat16)
    for number in range(STEP_HEADS):
        store(step, slot, number).start()

    @pl.when(step == steps - 1)
    def _():
        for number in range(STEP_HEADS):
            store(step, slot, number).wait()

    @pl.when((step == steps - 1) & (steps >= 2))
    def _():
        for number in range(STEP_HEADS):
            store(step - 1, 1 - slot, number).wait()


def spatial_piece(meta, first, count, queries, keys, values, keys_far, values_far, so_far):
    rows = queries.shape[0]
    operands, specs = [], []
    for number in range(STEP_HEADS):
        place = lambda i, meta, number=number: (0, meta[first + i * STEP_HEADS + number])
        operands += [queries, keys, values, keys_far, values_far]
        specs += [pl.BlockSpec((rows, HEAD_DIM), place)] * 5
    aliases = {}
    if so_far is not None:
        operands.append(so_far)
        specs.append(HBM)
        aliases = {len(operands): 0}
    return pl.pallas_call(
        functools.partial(spatial_kernel, math.log2(math.e) / math.sqrt(HEAD_DIM), first),
        out_shape=jax.ShapeDtypeStruct(queries.shape, jnp.bfloat16),
        grid_spec=pltpu.PrefetchScalarGridSpec(
            num_scalar_prefetch=1,
            grid=(count // STEP_HEADS,),
            in_specs=specs,
            out_specs=HBM,
            scratch_shapes=[
                pltpu.VMEM((2, STEP_HEADS, rows, HEAD_DIM), jnp.bfloat16),
                pltpu.SemaphoreType.DMA((2, STEP_HEADS)),
            ],
        ),
        input_output_aliases=aliases,
        compiler_params=pltpu.CompilerParams(vmem_limit_bytes=50 * MIB),
        cost_estimate=pl.CostEstimate(
            flops=count * rows * 2 * rows * HEAD_DIM * 4,
            bytes_accessed=count * 6 * rows * HEAD_DIM * 2,
            transcendentals=count * rows * 2 * rows,
        ),
        name="spatial_heads",
    )(meta, *operands)


def pack_kernel(reach, meta, own_a, low_a, own_b, low_b, for_a, for_b, sems):
    heads = (meta.shape[0] - 4 * TEMP_HEADS) // 3
    side, place = position()
    even = place % 2 == 0
    sources = (
        (jnp.where(even, place + reach - 1, place - reach + 1), own_a, low_a, for_b, sems.at[0]),
        (jnp.where(even, place - reach + 1, place + reach - 1), own_b, low_b, for_a, sems.at[1]),
    )

    def one_item(number, carry):
        item = meta[3 * heads + number]
        head, kind = item // 2, item % 2
        for origin, own, low, out, sem in sources:
            near = (origin < reach).astype(jnp.int32)
            is_own = (near + kind + side) % 2 == 0

            @pl.when(is_own)
            def _():
                pltpu.make_async_copy(own.at[HIGH + head], out.at[number], sem).start()

            @pl.when(jnp.logical_not(is_own))
            def _():
                pltpu.make_async_copy(low.at[head], out.at[number], sem).start()

        return carry

    lax.fori_loop(0, for_a.shape[0], one_item, jnp.int32(0))
    pltpu.make_async_copy(for_a, for_a, sems.at[1]).wait()
    pltpu.make_async_copy(for_b, for_b, sems.at[0]).wait()


def pack(meta, reach, size, own, low):
    out = jax.ShapeDtypeStruct((size,) + low[0].shape[1:], jnp.bfloat16)
    return pl.pallas_call(
        functools.partial(pack_kernel, reach),
        out_shape=(out, out),
        in_specs=[SMEM] + [HBM] * 4,
        out_specs=(VMEM, VMEM),
        scratch_shapes=[pltpu.SemaphoreType.DMA((2,))],
        compiler_params=pltpu.CompilerParams(vmem_limit_bytes=12 * MIB),
        name="pack_items",
    )(meta, own[0], low[0], own[1], low[1])


def temporal_kernel(scale, frames, reach, first_head, stores, meta, query_own, query_far, *rest):
    if stores:
        refs, (_, out, out_far, out_own, sem) = rest[:-5], rest[-5:]
    else:
        refs, (out_own, out_far) = rest[:-2], rest[-2:]
    count, half = out_far.shape[:2]
    is_high = first_head < HIGH
    heads = (meta.shape[0] - 4 * TEMP_HEADS) // 3
    first_listed = 0 if is_high else HIGH
    side, place = position()
    odd = place % 2 == 1
    size = PIXEL_BLOCK

    shifts = [jnp.int32(0)]
    for distance in range(1, reach):
        up = jnp.where(odd, -distance, distance)
        shifts += [up, -up]
    pairs, last = refs[: 2 * len(shifts)], refs[2 * len(shifts) :]
    lower = place < reach
    from_a = lower != odd
    if last:
        shifts.append(jnp.where(lower, reach, -reach))
    slots = 2 * len(shifts)
    row = lax.broadcasted_iota(jnp.int32, (2 * size, 1), 0)
    column = lax.broadcasted_iota(jnp.int32, (1, slots * size), 1)
    row_frame = jnp.where(row >= size, 1 - side, side) + 2 * place
    slot = column // size
    shift = jnp.zeros_like(slot)
    for number, step in enumerate(shifts):
        shift = jnp.where(slot // 2 == number, step, shift)
    first_of = side
    if last and not is_high:
        first_of = jnp.where(slot // 2 == len(shifts) - 1, jnp.where(lower, 0, 1), side)
    column_frame = jnp.where(slot % 2 == 1, 1 - first_of, first_of) + 2 * (place + shift)
    far = 4 * frames
    column_frame = jnp.where((column_frame >= 0) & (column_frame < frames), column_frame, far)
    apart = jnp.where(row % size == column % size, jnp.abs(row_frame - column_frame), far)
    parts = [slice(start, start + size) for start in range(0, half, size)]

    def one_head(number, carry):
        head = first_head + number
        keep = apart <= meta[2 * heads + head]

        def stacked(kind, part):
            blocks = [pair[head if pair.shape[0] == TEMP_HEADS else head - first_listed, kind, part, :] for pair in pairs]
            if is_high:
                for by_b, by_a in (last[:2], last[2:]):
                    blocks.append(jnp.where(from_a, by_a[head, kind, part, :], by_b[head, kind, part, :]))
            elif last:
                for which in range(2):
                    item = meta[3 * heads + 2 * TEMP_HEADS + 2 * (head - HIGH) + which]
                    item = jnp.minimum(item, last[0].shape[0] - 1)
                    by_a, by_b = (block[item, kind, part, :] for block in last)
                    blocks.append(jnp.where(from_a, by_a, by_b))
            return jnp.concatenate(blocks, axis=0)

        scores = []
        for part in parts:
            query = jnp.concatenate([query_own[head, part, :], query_far[head, part, :]], axis=0)
            score = lax.dot_general(
                query, stacked(0, part), (((1,), (1,)), ((), ())), preferred_element_type=jnp.float32
            )
            scores.append(jnp.where(keep, score, MASKED))
        weights = []
        for score in scores:
            peak = jnp.max(score, axis=1, keepdims=True)
            weight = jnp.exp2((score - peak) * scale)
            weights.append((weight.astype(jnp.bfloat16), jnp.sum(weight, axis=1, keepdims=True)))
        results = [
            jnp.dot(weight, stacked(1, part), preferred_element_type=jnp.float32) / total
            for part, (weight, total) in zip(parts, weights)
        ]
        for part, result in zip(parts, results):
            out_own[number, part, :] = result[:size].astype(jnp.bfloat16)
            out_far[number, part, :] = result[size:].astype(jnp.bfloat16)
        if stores:
            columns = columns_of(meta[heads + head])
            pltpu.make_async_copy(out_own.at[number], out.at[rows_of(side, half), columns], sem).start()
        return carry

    lax.fori_loop(0, count, one_head, jnp.int32(0))
    if stores:
        pltpu.make_async_copy(out_own, out_own, sem).wait()


def temporal(meta, frames, reach, heads, query_own, query_far, pairs, last, so_far=None):
    first_head, end = heads
    count, half = end - first_head, query_own.shape[1]
    stores = so_far is not None
    operands = [meta, query_own, query_far, *pairs, *last]
    specs = [SMEM] + [VMEM] * (len(operands) - 1)
    block = jax.ShapeDtypeStruct((count, half, HEAD_DIM), jnp.bfloat16)
    outs, out_specs, scratch = (block, block), (VMEM, VMEM), []
    if stores:
        operands.append(so_far)
        specs.append(HBM)
        outs, out_specs = (jax.ShapeDtypeStruct(so_far.shape, so_far.dtype), block), (HBM, VMEM)
        scratch = [pltpu.VMEM(block.shape, block.dtype), pltpu.SemaphoreType.DMA(())]
    slots = 2 + len(pairs)
    return pl.pallas_call(
        functools.partial(
            temporal_kernel, math.log2(math.e) / math.sqrt(HEAD_DIM), frames, reach, first_head, stores
        ),
        out_shape=outs,
        in_specs=specs,
        out_specs=out_specs,
        scratch_shapes=scratch,
        input_output_aliases={len(operands) - 1: 0} if stores else {},
        compiler_params=pltpu.CompilerParams(vmem_limit_bytes=44 * MIB),
        cost_estimate=pl.CostEstimate(
            flops=count * half * slots * PIXEL_BLOCK * HEAD_DIM * 8,
            bytes_accessed=count * half * HEAD_DIM * 2 * (4 + 2 * slots),
            transcendentals=count * half * 2 * slots * PIXEL_BLOCK,
        ),
        name="temporal_heads",
    )(*operands)


def finish_kernel(plan, meta, *refs):
    blocks, (_, out, sem) = refs[:-3], refs[-3:]
    heads = (meta.shape[0] - 4 * TEMP_HEADS) // 3
    side, _ = position()
    for block, (head, came_back) in zip(blocks, plan):
        count, half = block.shape[:2]
        rows = rows_of(1 - side if came_back else side, half)
        for number in range(count):
            columns = columns_of(meta[heads + head + number])
            pltpu.make_async_copy(block.at[number], out.at[rows, columns], sem).start()
    for block in blocks:
        pltpu.make_async_copy(block, block, sem).wait()


def finish(meta, parts, so_far):
    blocks = [block for block, _, _ in parts]
    return pl.pallas_call(
        functools.partial(finish_kernel, [(head, came_back) for _, head, came_back in parts]),
        out_shape=jax.ShapeDtypeStruct(so_far.shape, so_far.dtype),
        in_specs=[SMEM] + [VMEM] * len(blocks) + [HBM],
        out_specs=HBM,
        scratch_shapes=[pltpu.SemaphoreType.DMA(())],
        input_output_aliases={1 + len(blocks): 0},
        compiler_params=pltpu.CompilerParams(vmem_limit_bytes=4 * MIB),
        cost_estimate=pl.CostEstimate(flops=0, bytes_accessed=so_far.size // 2, transcendentals=0),
        name="finish",
    )(meta, *blocks, so_far)


def shards(queries, keys, values, labels, band):
    frames = lax.axis_size("frame") // 2
    reach = frames // 4

    keys_far = swap_bit(keys, 0)
    values_far = swap_bit(values, 0)
    meta, choice, pair_keep, high_send, low_send = extract(reach, labels, band, keys, values)

    def attend_piece(result, number):
        first, count = sum(SPATIAL_PIECES[:number]), SPATIAL_PIECES[number]
        return spatial_piece(meta, first, count, queries, keys, values, keys_far, values_far, result)

    def both_swaps(held, distance):
        return swap_pairs(held[1], 0, distance), swap_pairs(held[0], 1, distance)

    own = both_swaps((pair_keep, pair_keep), 1)
    high_got = swap_bit(high_send, 1)
    low_got = swap_bit(low_send, 1)
    result = attend_piece(None, 0)
    meta_then, result = lax.optimization_barrier((meta, result))
    query_keep, query_send = extract_queries(meta_then, queries)
    high_got, query_send, result = lax.optimization_barrier((high_got, query_send, result))
    high = both_swaps((high_got, high_got), 1)
    result = attend_piece(result, 1)
    own, low_got, query_send, choice, result = lax.optimization_barrier((own, low_got, query_send, choice, result))
    low = both_swaps((low_got, low_got), 1)
    high_pairs = [pair_keep, high_got, own[0], high[0], own[1], high[1]]
    low_pairs = [pair_keep, low_got, own[0], low[0], own[1], low[1]]
    for distance in range(2, reach):
        own, high, low = (both_swaps(held, distance) for held in (own, high, low))
        high_pairs += [own[0], high[0], own[1], high[1]]
        low_pairs += [own[0], low[0], own[1], low[1]]
    own_last = both_swaps((own[0][:HIGH], own[1][:HIGH]), reach)
    own_last = own_last[::-1]
    high, result = lax.optimization_barrier((high, result))
    choice = largest(choice)
    query_got = swap_bit(query_send, 1)
    result = attend_piece(result, 2)
    own, high, low, own_last, query_got, choice, result = lax.optimization_barrier(
        (own, high, low, own_last, query_got, choice, result)
    )

    def last_swaps(size, result, meta, own, high, low, own_last, query_keep, query_got, high_pairs, low_pairs):
        attend = functools.partial(temporal, meta, frames, reach)
        high_last = both_swaps(high, reach)
        with_items = min(HIGH + size, TEMP_HEADS)
        parts = []
        if with_items < TEMP_HEADS:
            result, send = attend((with_items, TEMP_HEADS), query_keep, query_got, low_pairs, [], result)
            parts.append((swap_bit(send, 1), with_items, True))
            meta_then, query_keep, _ = lax.optimization_barrier((meta, query_keep, send))
        else:
            meta_then = meta
        if size:
            for_a, for_b = pack(meta_then, reach, size, own, low)
            items = [swap_pairs(for_a, 0, reach), swap_pairs(for_b, 1, reach)]
        keep, send = attend((0, HIGH), query_keep, query_got, high_pairs, [*own_last, *high_last[::-1]])
        parts += [(keep, 0, False), (swap_bit(send, 1), 0, True)]
        if size:
            query_keep, *_ = lax.optimization_barrier((query_keep, send, [block for block, _, _ in parts[:-1]]))
            keep, send = attend((HIGH, with_items), query_keep, query_got, low_pairs, items)
            parts += [(keep, HIGH, False), (swap_bit(send, 1), HIGH, True)]
        return finish(meta, parts, result)

    return lax.switch(
        choice[0], [functools.partial(last_swaps, size) for size in LEVELS],
        result, meta, own, high, low, own_last, query_keep, query_got, high_pairs, low_pairs,
    )


def solution(mesh):
    placed = (
        P(("group", "frame"), None),
        P(("group", "frame"), None),
        P(("group", "frame"), None),
        P("group"),
        P("group"),
    )
    return jax.shard_map(
        shards, mesh=mesh, in_specs=placed, out_specs=P(("group", "frame"), None), check_vma=False
    )
```

profile of v0, /device:TPU:0, one launch (start us, length us, event | category | flops | bytes accessed | tf_op | source)
XLA Modules:
  0.0 83.2 jit_solution(8714184846381061277)
XLA Ops:
  0.0 0.5 collective-permute-start.47
  0.5 0.1 collective-permute-start.48
  0.5 3.4 %extract_temporal.1 = (s32[160]{0:T(256)S(1)}, s32[1]{0:T(128)}, bf16[10,2,160,128]{3,2,1,0:T(8,128)(2,1)S(1)}, bf16[5,2,160,128]{3,2,1,0:T(8,128)(2,1)}, bf16[5,2,160,128]{3,2,1,0:T(8,128)(2,1)}) custom-call(s32[40]{0:T(128)} %labels_hbm.1, s32[40]{0:T(128)} %band_hbm.1, bf16[320,5120]{1,0:T(8,128)(2,1)} %refs_11_.5, bf16[320,5120]{1,0:T(8,128)(2,1)} %refs_12_.5), custom_call_target="tpu_custom_call" | custom-call | bytes 3276800 | tf_op jit(solution)/shard_map/extract_temporal/pallas_call | solution.py:137
  4.0 0.7 collective-permute-start.44
  4.7 5.9 %collective-permute-start.43 = (bf16[10,2,160,128]{3,2,1,0:T(8,128)(2,1)S(1)}, bf16[10,2,160,128]{3,2,1,0:T(8,128)(2,1)S(1)}, u32[]{:S(2)}, u32[]{:S(2)}) collective-permute-start(bf16[10,2,160,128]{3,2,1,0:T(8,128)(2,1)S(1)} %get-tuple-element.533), channel_id=1, source_target_pairs={{0,4},{1,5},{2,6},{3,7},{4,0},{5,1},{6,2},{7,3},{8,12},{9,13},{10,... | collective-permute-start | bytes 2457608 | tf_op jit(solution)/shard_map/ppermute | solution.py:39
  10.5 1.5 %collective-permute-start.46 = (bf16[5,2,160,128]{3,2,1,0:T(8,128)(2,1)}, bf16[5,2,160,128]{3,2,1,0:T(8,128)(2,1)S(1)}, u32[]{:S(2)}, u32[]{:S(2)}) collective-permute-start(bf16[5,2,160,128]{3,2,1,0:T(8,128)(2,1)} %get-tuple-element.535), channel_id=1, source_target_pairs={{0,2},{1,3},{2,0},{3,1},{4,6},{5,7},{6,4},{7,5},{8,10},{9,11},{10,... | collective-permute-start | bytes 1228808 | tf_op jit(solution)/shard_map/ppermute | solution.py:27
  12.1 0.0 collective-permute-done.47.refs_3_.refs_8_.refs_13_
  12.1 0.5 collective-permute-start.45
  12.6 6.0 %spatial_heads.3.refs_15_ = bf16[320,5120]{1,0:T(8,128)(2,1)S(1)} custom-call(s32[160]{0:T(256)S(1)} %get-tuple-element.537.meta, bf16[320,5120]{1,0:T(8,128)(2,1)S(1)} %copy-done, bf16[320,5120]{1,0:T(8,128)(2,1)} %refs_11_.5, bf16[320,5120]{1,0:T(8,128)(2,1)} %refs_12_.5, bf16[320,5120]{1,0:T(8,128)(2,1)} %collective-permute-done.47.refs_3_.refs_8_.refs_13_, ...), custom_call_target="tpu_custom_call" | custom-call | flops 943718400 | bytes 4423680 | tf_op jit(solution)/shard_map/spatial_heads/pallas_call | solution.py:244
  18.6 0.9 %extract_queries.1 = (bf16[10,160,128]{2,1,0:T(8,128)(2,1)S(1)}, bf16[10,160,128]{2,1,0:T(8,128)(2,1)S(1)}) custom-call(s32[160]{0:T(256)S(1)} %get-tuple-element.537.meta, bf16[320,5120]{1,0:T(8,128)(2,1)S(1)} %copy-done), custom_call_target="tpu_custom_call" | custom-call | bytes 1638400 | tf_op jit(solution)/shard_map/extract_queries/pallas_call | solution.py:174
  19.5 3.7 %collective-permute-done.46 = bf16[5,2,160,128]{3,2,1,0:T(8,128)(2,1)S(1)} collective-permute-done((bf16[5,2,160,128]{3,2,1,0:T(8,128)(2,1)}, bf16[5,2,160,128]{3,2,1,0:T(8,128)(2,1)S(1)}, u32[]{:S(2)}, u32[]{:S(2)}) %collective-permute-start.46) | collective-permute-done | bytes 409632 | tf_op jit(solution)/shard_map/ppermute | solution.py:27
  23.2 0.7 collective-permute-start.50
  23.8 1.8 %collective-permute-start.49 = (bf16[5,2,160,128]{3,2,1,0:T(8,128)(2,1)S(1)}, bf16[5,2,160,128]{3,2,1,0:T(8,128)(2,1)S(1)}, u32[]{:S(2)}, u32[]{:S(2)}) collective-permute-start(bf16[5,2,160,128]{3,2,1,0:T(8,128)(2,1)S(1)} %collective-permute-done.46), channel_id=1, source_target_pairs={{0,4},{1,5},{2,6},{3,7},{4,0},{5,1},{6,2},{7,3},{8,12},{9,13},{10,... | collective-permute-start | bytes 1228808 | tf_op jit(solution)/shard_map/ppermute | solution.py:39
  25.6 4.5 %spatial_heads.4.refs_15_ = bf16[320,5120]{1,0:T(8,128)(2,1)S(1)} custom-call(s32[160]{0:T(256)S(1)} %get-tuple-element.537.meta, bf16[320,5120]{1,0:T(8,128)(2,1)S(1)} %copy-done, bf16[320,5120]{1,0:T(8,128)(2,1)} %refs_11_.5, bf16[320,5120]{1,0:T(8,128)(2,1)} %refs_12_.5, ...), custom_call_target="tpu_custom_call", output_to_operand_aliasing={{}: (16, {})} | custom-call | flops 629145600 | bytes 2949120 | tf_op jit(solution)/shard_map/spatial_heads/pallas_call | solution.py:244
  30.2 0.3 collective-permute-done.45
  30.4 0.0 collective-permute-done.44
  30.4 0.0 collective-permute-done.43
  30.4 1.5 %collective-permute-start.56 = (s32[1]{0:T(128)}, s32[1]{0:T(128)}, u32[]{:S(2)}, u32[]{:S(2)}) collective-permute-start(s32[1]{0:T(128)} %get-tuple-element.551), channel_id=1, source_target_pairs={{0,16},{16,0},{1,17},{17,1},{2,18},{18,2},{3,19},{19,3},{4,20},{20... | collective-permute-start | bytes 20 | tf_op jit(solution)/shard_map/ppermute | solution.py:47
  32.0 1.3 %collective-permute-start.54 = (bf16[5,2,160,128]{3,2,1,0:T(8,128)(2,1)S(1)}, bf16[5,2,160,128]{3,2,1,0:T(8,128)(2,1)S(1)}, u32[]{:S(2)}, u32[]{:S(2)}) collective-permute-start(bf16[5,2,160,128]{3,2,1,0:T(8,128)(2,1)S(1)} %slice.7), channel_id=1, source_target_pairs={{4,0},{5,1},{6,2},{7,3},{8,12},{9,13},{10,14},{11,15},{20,16},{21,... | collective-permute-start | bytes 1228808 | tf_op jit(solution)/shard_map/ppermute | solution.py:39
  33.3 0.7 collective-permute-start.53
  34.0 0.3 collective-permute-done.56
  34.3 1.5 %collective-permute-start.55 = (bf16[10,160,128]{2,1,0:T(8,128)(2,1)S(1)}, bf16[10,160,128]{2,1,0:T(8,128)(2,1)S(1)}, u32[]{:S(2)}, u32[]{:S(2)}) collective-permute-start(bf16[10,160,128]{2,1,0:T(8,128)(2,1)S(1)} %get-tuple-element.550), channel_id=1, source_target_pairs={{0,2},{1,3},{2,0},{3,1},{4,6},{5,7},{6,4},{7,5},{8,10},{9,11},{10,... | collective-permute-start | bytes 1228808 | tf_op jit(solution)/shard_map/ppermute | solution.py:27
  35.8 0.0 collective-permute-done.50
  35.8 0.7 collective-permute-start.52
  36.5 1.9 %collective-permute-done.49 = bf16[5,2,160,128]{3,2,1,0:T(8,128)(2,1)S(1)} collective-permute-done((bf16[5,2,160,128]{3,2,1,0:T(8,128)(2,1)S(1)}, bf16[5,2,160,128]{3,2,1,0:T(8,128)(2,1)S(1)}, u32[]{:S(2)}, u32[]{:S(2)}) %collective-permute-start.49) | collective-permute-done | bytes 409632 | tf_op jit(solution)/shard_map/ppermute | solution.py:39
  38.4 5.1 %collective-permute-start.51 = (bf16[5,2,160,128]{3,2,1,0:T(8,128)(2,1)S(1)}, bf16[5,2,160,128]{3,2,1,0:T(8,128)(2,1)S(1)}, u32[]{:S(2)}, u32[]{:S(2)}) collective-permute-start(bf16[5,2,160,128]{3,2,1,0:T(8,128)(2,1)S(1)} %collective-permute-done.45), channel_id=1, source_target_pairs={{0,4},{1,5},{2,6},{3,7},{4,0},{5,1},{6,2},{7,3},{8,12},{9,13},{10,... | collective-permute-start | bytes 1228808 | tf_op jit(solution)/shard_map/ppermute | solution.py:39
  44.6 8.9 %spatial_heads.5 = bf16[320,5120]{1,0:T(8,128)(2,1)S(1)} custom-call(s32[160]{0:T(256)S(1)} %get-tuple-element.537.meta, bf16[320,5120]{1,0:T(8,128)(2,1)S(1)} %copy-done, bf16[320,5120]{1,0:T(8,128)(2,1)} %refs_11_.5, bf16[320,5120]{1,0:T(8,128)(2,1)} %refs_12_.5, ...), custom_call_target="tpu_custom_call", output_to_operand_aliasing={{}: (16, {})} | custom-call | flops 1572864000 | bytes 7372800 | tf_op jit(solution)/shard_map/spatial_heads/pallas_call | solution.py:244
  53.6 0.0 collective-permute-done.54
  53.6 0.0 collective-permute-done.55
  53.6 0.0 collective-permute-done.52
  53.6 1.5 %collective-permute-done.51 = bf16[5,2,160,128]{3,2,1,0:T(8,128)(2,1)S(1)} collective-permute-done((bf16[5,2,160,128]{3,2,1,0:T(8,128)(2,1)S(1)}, bf16[5,2,160,128]{3,2,1,0:T(8,128)(2,1)S(1)}, u32[]{:S(2)}, u32[]{:S(2)}) %collective-permute-start.51) | collective-permute-done | bytes 409632 | tf_op jit(solution)/shard_map/ppermute | solution.py:39
  55.1 26.4 %conditional.1 = (bf16[320,5120]{1,0:T(8,128)(2,1)S(1)}) conditional(s32[]{:T(128)} %bitcast, (s32[160]{0:T(256)S(1)}, bf16[10,160,128]{2,1,0:T(8,128)(2,1)S(1)}, bf16[10,160,128]{2,1,0:T(8,128)(2,1)S(1)}, bf16[10,2,160,128]{3,2,1,0:T(8,128)(2,1)S(1)}, bf16[5,2,160,128]{3,2,1,0:T(8,128)(2,1)S(1)}, ...), branch_computations={%region_0.0_spmd, %region_1.0_spmd, %region_2.0_spmd, %region_3.0_... | conditional | flops 419430400 | bytes 20480248 | solution.py:523
  55.1 0.7 collective-permute-start.5
  55.8 1.3 %collective-permute-start.6 = (bf16[5,2,160,128]{3,2,1,0:T(8,128)(2,1)S(1)}, bf16[5,2,160,128]{3,2,1,0:T(8,128)(2,1)S(1)}, u32[]{:S(2)}, u32[]{:S(2)}) collective-permute-start(bf16[5,2,160,128]{3,2,1,0:T(8,128)(2,1)S(1)} %get-tuple-element.335.rest_5_), channel_id=1, source_target_pairs={{4,0},{5,1},{6,2},{7,3},{8,12},{9,13},{10,14},{11,15},{20,16},{21,... | collective-permute-start | bytes 1228808 | tf_op jit(solution)/shard_map/cond/branch_1_fun/ppermute | solution.py:39
  57.1 2.2 %temporal_heads.19 = (bf16[320,5120]{1,0:T(8,128)(2,1)S(1)}, bf16[3,160,128]{2,1,0:T(8,128)(2,1)S(1)}) custom-call(s32[160]{0:T(256)S(1)} %get-tuple-element.343.meta, bf16[10,160,128]{2,1,0:T(8,128)(2,1)S(1)} %get-tuple-element.342.query_own, bf16[10,160,128]{2,1,0:T(8,128)(2,1)S(1)} %get-tuple-element.323.query_far, ...), custom_call_target="tpu_custom_call", output_to_operand_aliasing={{0}: (9, {})} | custom-call | flops 125829120 | bytes 2457600 | tf_op jit(solution)/shard_map/cond/branch_1_fun/temporal_heads/pallas_call | solution.py:411
  59.2 1.1 %pack_items.6 = (bf16[2,2,160,128]{3,2,1,0:T(8,128)(2,1)S(1)}, bf16[2,2,160,128]{3,2,1,0:T(8,128)(2,1)S(1)}) custom-call(s32[160]{0:T(256)S(1)} %get-tuple-element.343.meta, bf16[10,2,160,128]{3,2,1,0:T(8,128)(2,1)S(1)} %get-tuple-element.344.own_a, bf16[5,2,160,128]{3,2,1,0:T(8,128)(2,1)S(1)} %get-tuple-element.345.low_a, ...), custom_call_target="tpu_custom_call" | custom-call | tf_op jit(solution)/shard_map/cond/branch_1_fun/pack_items/pallas_call | solution.py:301
  60.3 1.3 %collective-permute-start.8 = (bf16[2,2,160,128]{3,2,1,0:T(8,128)(2,1)S(1)}, bf16[2,2,160,128]{3,2,1,0:T(8,128)(2,1)S(1)}, u32[]{:S(2)}, u32[]{:S(2)}) collective-permute-start(bf16[2,2,160,128]{3,2,1,0:T(8,128)(2,1)S(1)} %get-tuple-element.348), channel_id=1, source_target_pairs={{4,0},{5,1},{6,2},{7,3},{8,12},{9,13},{10,14},{11,15},{20,16},{21,... | collective-permute-start | bytes 491528 | tf_op jit(solution)/shard_map/cond/branch_1_fun/ppermute | solution.py:39
  61.6 0.7 collective-permute-start.9
  62.3 1.6 %collective-permute-start.4 = (bf16[3,160,128]{2,1,0:T(8,128)(2,1)S(1)}, bf16[3,160,128]{2,1,0:T(8,128)(2,1)S(1)}, u32[]{:S(2)}, u32[]{:S(2)}) collective-permute-start(bf16[3,160,128]{2,1,0:T(8,128)(2,1)S(1)} %get-tuple-element.331), channel_id=1, source_target_pairs={{0,2},{1,3},{2,0},{3,1},{4,6},{5,7},{6,4},{7,5},{8,10},{9,11},{10,... | collective-permute-start | bytes 368648 | tf_op jit(solution)/shard_map/cond/branch_1_fun/ppermute | solution.py:27
  63.9 6.1 %collective-permute-done.6.rest_9_ = bf16[5,2,160,128]{3,2,1,0:T(8,128)(2,1)S(1)} collective-permute-done((bf16[5,2,160,128]{3,2,1,0:T(8,128)(2,1)S(1)}, bf16[5,2,160,128]{3,2,1,0:T(8,128)(2,1)S(1)}, u32[]{:S(2)}, u32[]{:S(2)}) %collective-permute-start.6) | collective-permute-done | bytes 409632 | tf_op jit(solution)/shard_map/cond/branch_1_fun/ppermute | solution.py:39
  70.0 2.9 %temporal_heads.20 = (bf16[5,160,128]{2,1,0:T(8,128)(2,1)S(1)}, bf16[5,160,128]{2,1,0:T(8,128)(2,1)S(1)}) custom-call(s32[160]{0:T(256)S(1)} %get-tuple-element.343.meta, bf16[10,160,128]{2,1,0:T(8,128)(2,1)S(1)} %get-tuple-element.342.query_own, bf16[10,160,128]{2,1,0:T(8,128)(2,1)S(1)} %get-tuple-element.323.query_far, ...), custom_call_target="tpu_custom_call" | custom-call | flops 209715200 | bytes 4096000 | tf_op jit(solution)/shard_map/cond/branch_1_fun/temporal_heads/pallas_call | solution.py:411
  72.9 1.6 %collective-permute-start.7 = (bf16[5,160,128]{2,1,0:T(8,128)(2,1)S(1)}, bf16[5,160,128]{2,1,0:T(8,128)(2,1)S(1)}, u32[]{:S(2)}, u32[]{:S(2)}) collective-permute-start(bf16[5,160,128]{2,1,0:T(8,128)(2,1)S(1)} %get-tuple-element.341), channel_id=1, source_target_pairs={{0,2},{1,3},{2,0},{3,1},{4,6},{5,7},{6,4},{7,5},{8,10},{9,11},{10,... | collective-permute-start | bytes 614408 | tf_op jit(solution)/shard_map/cond/branch_1_fun/ppermute | solution.py:27
  74.5 1.5 %temporal_heads.21 = (bf16[2,160,128]{2,1,0:T(8,128)(2,1)S(1)}, bf16[2,160,128]{2,1,0:T(8,128)(2,1)S(1)}) custom-call(s32[160]{0:T(256)S(1)} %get-tuple-element.343.meta, bf16[10,160,128]{2,1,0:T(8,128)(2,1)S(1)} %get-tuple-element.342.query_own, bf16[10,160,128]{2,1,0:T(8,128)(2,1)S(1)} %get-tuple-element.323.query_far, ...), custom_call_target="tpu_custom_call" | custom-call | flops 83886080 | bytes 1638400 | tf_op jit(solution)/shard_map/cond/branch_1_fun/temporal_heads/pallas_call | solution.py:411
  76.0 0.6 collective-permute-start.10
  76.6 3.9 %collective-permute-done.10.refs_4_ = bf16[2,160,128]{2,1,0:T(8,128)(2,1)S(1)} collective-permute-done((bf16[2,160,128]{2,1,0:T(8,128)(2,1)S(1)}, bf16[2,160,128]{2,1,0:T(8,128)(2,1)S(1)}, u32[]{:S(2)}, u32[]{:S(2)}) %collective-permute-start.10) | collective-permute-done | bytes 81952 | tf_op jit(solution)/shard_map/cond/branch_1_fun/ppermute | solution.py:27
  80.5 0.8 finish.8
  81.5 0.0 copy-start.1
  81.5 1.7 %copy-done.1 = bf16[320,5120]{1,0:T(8,128)(2,1)} copy-done((bf16[320,5120]{1,0:T(8,128)(2,1)}, bf16[320,5120]{1,0:T(8,128)(2,1)S(1)}, u32[]{:S(2)}) %copy-start.1) | copy-done | bytes 3276824
  (11 shorter events, 0.1 us)
Async XLA Ops:
  0.0 12.6 %copy-start = (bf16[320,5120]{1,0:T(8,128)(2,1)S(1)}, bf16[320,5120]{1,0:T(8,128)(2,1)}, u32[]{:S(2)}) copy-start(bf16[320,5120]{1,0:T(8,128)(2,1)} %refs_10_.5) | copy-start | bytes 9830404
  0.0 12.1 %collective-permute-start.47 = (bf16[320,5120]{1,0:T(8,128)(2,1)}, bf16[320,5120]{1,0:T(8,128)(2,1)}, u32[]{:S(2)}, u32[]{:S(2)}) collective-permute-start(bf16[320,5120]{1,0:T(8,128)(2,1)} %refs_11_.5), channel_id=1, source_target_pairs={{0,1},{1,0},{2,3},{3,2},{4,5},{5,4},{6,7},{7,6},{8,9},{9,8},{10,11... | collective-permute-start | bytes 9830408 | tf_op jit(solution)/shard_map/ppermute | solution.py:27
  0.5 12.1 %collective-permute-start.48 = (bf16[320,5120]{1,0:T(8,128)(2,1)}, bf16[320,5120]{1,0:T(8,128)(2,1)}, u32[]{:S(2)}, u32[]{:S(2)}) collective-permute-start(bf16[320,5120]{1,0:T(8,128)(2,1)} %refs_12_.5), channel_id=1, source_target_pairs={{0,1},{1,0},{2,3},{3,2},{4,5},{5,4},{6,7},{7,6},{8,9},{9,8},{10,11... | collective-permute-start | bytes 9830408 | tf_op jit(solution)/shard_map/ppermute | solution.py:27
  4.0 26.4 %collective-permute-start.44 = (bf16[10,2,160,128]{3,2,1,0:T(8,128)(2,1)S(1)}, bf16[10,2,160,128]{3,2,1,0:T(8,128)(2,1)S(1)}, u32[]{:S(2)}, u32[]{:S(2)}) collective-permute-start(bf16[10,2,160,128]{3,2,1,0:T(8,128)(2,1)S(1)} %get-tuple-element.533), channel_id=1, source_target_pairs={{4,8},{5,9},{6,10},{7,11},{8,4},{9,5},{10,6},{11,7},{20,24},{21,25... | collective-permute-start | bytes 2457608 | tf_op jit(solution)/shard_map/ppermute | solution.py:39
  4.7 25.7 %collective-permute-start.43 = (bf16[10,2,160,128]{3,2,1,0:T(8,128)(2,1)S(1)}, bf16[10,2,160,128]{3,2,1,0:T(8,128)(2,1)S(1)}, u32[]{:S(2)}, u32[]{:S(2)}) collective-permute-start(bf16[10,2,160,128]{3,2,1,0:T(8,128)(2,1)S(1)} %get-tuple-element.533), channel_id=1, source_target_pairs={{0,4},{1,5},{2,6},{3,7},{4,0},{5,1},{6,2},{7,3},{8,12},{9,13},{10,... | collective-permute-start | bytes 2457608 | tf_op jit(solution)/shard_map/ppermute | solution.py:39
  10.5 12.6 %collective-permute-start.46 = (bf16[5,2,160,128]{3,2,1,0:T(8,128)(2,1)}, bf16[5,2,160,128]{3,2,1,0:T(8,128)(2,1)S(1)}, u32[]{:S(2)}, u32[]{:S(2)}) collective-permute-start(bf16[5,2,160,128]{3,2,1,0:T(8,128)(2,1)} %get-tuple-element.535), channel_id=1, source_target_pairs={{0,2},{1,3},{2,0},{3,1},{4,6},{5,7},{6,4},{7,5},{8,10},{9,11},{10,... | collective-permute-start | bytes 1228808 | tf_op jit(solution)/shard_map/ppermute | solution.py:27
  12.1 18.3 %collective-permute-start.45 = (bf16[5,2,160,128]{3,2,1,0:T(8,128)(2,1)}, bf16[5,2,160,128]{3,2,1,0:T(8,128)(2,1)S(1)}, u32[]{:S(2)}, u32[]{:S(2)}) collective-permute-start(bf16[5,2,160,128]{3,2,1,0:T(8,128)(2,1)} %get-tuple-element.534), channel_id=1, source_target_pairs={{0,2},{1,3},{2,0},{3,1},{4,6},{5,7},{6,4},{7,5},{8,10},{9,11},{10,... | collective-permute-start | bytes 1228808 | tf_op jit(solution)/shard_map/ppermute | solution.py:27
  23.2 12.6 %collective-permute-start.50 = (bf16[5,2,160,128]{3,2,1,0:T(8,128)(2,1)S(1)}, bf16[5,2,160,128]{3,2,1,0:T(8,128)(2,1)S(1)}, u32[]{:S(2)}, u32[]{:S(2)}) collective-permute-start(bf16[5,2,160,128]{3,2,1,0:T(8,128)(2,1)S(1)} %collective-permute-done.46), channel_id=1, source_target_pairs={{4,8},{5,9},{6,10},{7,11},{8,4},{9,5},{10,6},{11,7},{20,24},{21,25... | collective-permute-start | bytes 1228808 | tf_op jit(solution)/shard_map/ppermute | solution.py:39
  23.8 14.6 %collective-permute-start.49 = (bf16[5,2,160,128]{3,2,1,0:T(8,128)(2,1)S(1)}, bf16[5,2,160,128]{3,2,1,0:T(8,128)(2,1)S(1)}, u32[]{:S(2)}, u32[]{:S(2)}) collective-permute-start(bf16[5,2,160,128]{3,2,1,0:T(8,128)(2,1)S(1)} %collective-permute-done.46), channel_id=1, source_target_pairs={{0,4},{1,5},{2,6},{3,7},{4,0},{5,1},{6,2},{7,3},{8,12},{9,13},{10,... | collective-permute-start | bytes 1228808 | tf_op jit(solution)/shard_map/ppermute | solution.py:39
  30.4 3.9 %collective-permute-start.56 = (s32[1]{0:T(128)}, s32[1]{0:T(128)}, u32[]{:S(2)}, u32[]{:S(2)}) collective-permute-start(s32[1]{0:T(128)} %get-tuple-element.551), channel_id=1, source_target_pairs={{0,16},{16,0},{1,17},{17,1},{2,18},{18,2},{3,19},{19,3},{4,20},{20... | collective-permute-start | bytes 20 | tf_op jit(solution)/shard_map/ppermute | solution.py:47
  32.0 21.6 %collective-permute-start.54 = (bf16[5,2,160,128]{3,2,1,0:T(8,128)(2,1)S(1)}, bf16[5,2,160,128]{3,2,1,0:T(8,128)(2,1)S(1)}, u32[]{:S(2)}, u32[]{:S(2)}) collective-permute-start(bf16[5,2,160,128]{3,2,1,0:T(8,128)(2,1)S(1)} %slice.7), channel_id=1, source_target_pairs={{4,0},{5,1},{6,2},{7,3},{8,12},{9,13},{10,14},{11,15},{20,16},{21,... | collective-permute-start | bytes 1228808 | tf_op jit(solution)/shard_map/ppermute | solution.py:39
  33.3 20.3 %collective-permute-start.53 = (bf16[5,2,160,128]{3,2,1,0:T(8,128)(2,1)S(1)}, bf16[5,2,160,128]{3,2,1,0:T(8,128)(2,1)S(1)}, u32[]{:S(2)}, u32[]{:S(2)}) collective-permute-start(bf16[5,2,160,128]{3,2,1,0:T(8,128)(2,1)S(1)} %slice.6), channel_id=1, source_target_pairs={{4,8},{5,9},{6,10},{7,11},{8,4},{9,5},{10,6},{11,7},{20,24},{21,25... | collective-permute-start | bytes 1228808 | tf_op jit(solution)/shard_map/ppermute | solution.py:39
  34.3 19.3 %collective-permute-start.55 = (bf16[10,160,128]{2,1,0:T(8,128)(2,1)S(1)}, bf16[10,160,128]{2,1,0:T(8,128)(2,1)S(1)}, u32[]{:S(2)}, u32[]{:S(2)}) collective-permute-start(bf16[10,160,128]{2,1,0:T(8,128)(2,1)S(1)} %get-tuple-element.550), channel_id=1, source_target_pairs={{0,2},{1,3},{2,0},{3,1},{4,6},{5,7},{6,4},{7,5},{8,10},{9,11},{10,... | collective-permute-start | bytes 1228808 | tf_op jit(solution)/shard_map/ppermute | solution.py:27
  35.8 17.8 %collective-permute-start.52 = (bf16[5,2,160,128]{3,2,1,0:T(8,128)(2,1)S(1)}, bf16[5,2,160,128]{3,2,1,0:T(8,128)(2,1)S(1)}, u32[]{:S(2)}, u32[]{:S(2)}) collective-permute-start(bf16[5,2,160,128]{3,2,1,0:T(8,128)(2,1)S(1)} %collective-permute-done.45), channel_id=1, source_target_pairs={{4,8},{5,9},{6,10},{7,11},{8,4},{9,5},{10,6},{11,7},{20,24},{21,25... | collective-permute-start | bytes 1228808 | tf_op jit(solution)/shard_map/ppermute | solution.py:39
  38.4 16.7 %collective-permute-start.51 = (bf16[5,2,160,128]{3,2,1,0:T(8,128)(2,1)S(1)}, bf16[5,2,160,128]{3,2,1,0:T(8,128)(2,1)S(1)}, u32[]{:S(2)}, u32[]{:S(2)}) collective-permute-start(bf16[5,2,160,128]{3,2,1,0:T(8,128)(2,1)S(1)} %collective-permute-done.45), channel_id=1, source_target_pairs={{0,4},{1,5},{2,6},{3,7},{4,0},{5,1},{6,2},{7,3},{8,12},{9,13},{10,... | collective-permute-start | bytes 1228808 | tf_op jit(solution)/shard_map/ppermute | solution.py:39
  55.1 8.8 %collective-permute-start.5 = (bf16[5,2,160,128]{3,2,1,0:T(8,128)(2,1)S(1)}, bf16[5,2,160,128]{3,2,1,0:T(8,128)(2,1)S(1)}, u32[]{:S(2)}, u32[]{:S(2)}) collective-permute-start(bf16[5,2,160,128]{3,2,1,0:T(8,128)(2,1)S(1)} %get-tuple-element.334.rest_3_), channel_id=1, source_target_pairs={{4,8},{5,9},{6,10},{7,11},{8,4},{9,5},{10,6},{11,7},{20,24},{21,25... | collective-permute-start | bytes 1228808 | tf_op jit(solution)/shard_map/cond/branch_1_fun/ppermute | solution.py:39
  55.8 14.2 %collective-permute-start.6 = (bf16[5,2,160,128]{3,2,1,0:T(8,128)(2,1)S(1)}, bf16[5,2,160,128]{3,2,1,0:T(8,128)(2,1)S(1)}, u32[]{:S(2)}, u32[]{:S(2)}) collective-permute-start(bf16[5,2,160,128]{3,2,1,0:T(8,128)(2,1)S(1)} %get-tuple-element.335.rest_5_), channel_id=1, source_target_pairs={{4,0},{5,1},{6,2},{7,3},{8,12},{9,13},{10,14},{11,15},{20,16},{21,... | collective-permute-start | bytes 1228808 | tf_op jit(solution)/shard_map/cond/branch_1_fun/ppermute | solution.py:39
  60.3 14.2 %collective-permute-start.8 = (bf16[2,2,160,128]{3,2,1,0:T(8,128)(2,1)S(1)}, bf16[2,2,160,128]{3,2,1,0:T(8,128)(2,1)S(1)}, u32[]{:S(2)}, u32[]{:S(2)}) collective-permute-start(bf16[2,2,160,128]{3,2,1,0:T(8,128)(2,1)S(1)} %get-tuple-element.348), channel_id=1, source_target_pairs={{4,0},{5,1},{6,2},{7,3},{8,12},{9,13},{10,14},{11,15},{20,16},{21,... | collective-permute-start | bytes 491528 | tf_op jit(solution)/shard_map/cond/branch_1_fun/ppermute | solution.py:39
  61.6 12.9 %collective-permute-start.9 = (bf16[2,2,160,128]{3,2,1,0:T(8,128)(2,1)S(1)}, bf16[2,2,160,128]{3,2,1,0:T(8,128)(2,1)S(1)}, u32[]{:S(2)}, u32[]{:S(2)}) collective-permute-start(bf16[2,2,160,128]{3,2,1,0:T(8,128)(2,1)S(1)} %get-tuple-element.349), channel_id=1, source_target_pairs={{4,8},{5,9},{6,10},{7,11},{8,4},{9,5},{10,6},{11,7},{20,24},{21,25... | collective-permute-start | bytes 491528 | tf_op jit(solution)/shard_map/cond/branch_1_fun/ppermute | solution.py:39
  62.3 12.2 %collective-permute-start.4 = (bf16[3,160,128]{2,1,0:T(8,128)(2,1)S(1)}, bf16[3,160,128]{2,1,0:T(8,128)(2,1)S(1)}, u32[]{:S(2)}, u32[]{:S(2)}) collective-permute-start(bf16[3,160,128]{2,1,0:T(8,128)(2,1)S(1)} %get-tuple-element.331), channel_id=1, source_target_pairs={{0,2},{1,3},{2,0},{3,1},{4,6},{5,7},{6,4},{7,5},{8,10},{9,11},{10,... | collective-permute-start | bytes 368648 | tf_op jit(solution)/shard_map/cond/branch_1_fun/ppermute | solution.py:27
  72.9 7.6 %collective-permute-start.7 = (bf16[5,160,128]{2,1,0:T(8,128)(2,1)S(1)}, bf16[5,160,128]{2,1,0:T(8,128)(2,1)S(1)}, u32[]{:S(2)}, u32[]{:S(2)}) collective-permute-start(bf16[5,160,128]{2,1,0:T(8,128)(2,1)S(1)} %get-tuple-element.341), channel_id=1, source_target_pairs={{0,2},{1,3},{2,0},{3,1},{4,6},{5,7},{6,4},{7,5},{8,10},{9,11},{10,... | collective-permute-start | bytes 614408 | tf_op jit(solution)/shard_map/cond/branch_1_fun/ppermute | solution.py:27
  76.0 4.5 %collective-permute-start.10 = (bf16[2,160,128]{2,1,0:T(8,128)(2,1)S(1)}, bf16[2,160,128]{2,1,0:T(8,128)(2,1)S(1)}, u32[]{:S(2)}, u32[]{:S(2)}) collective-permute-start(bf16[2,160,128]{2,1,0:T(8,128)(2,1)S(1)} %get-tuple-element.351), channel_id=1, source_target_pairs={{0,2},{1,3},{2,0},{3,1},{4,6},{5,7},{6,4},{7,5},{8,10},{9,11},{10,... | collective-permute-start | bytes 245768 | tf_op jit(solution)/shard_map/cond/branch_1_fun/ppermute | solution.py:27
  81.5 1.7 %copy-start.1 = (bf16[320,5120]{1,0:T(8,128)(2,1)}, bf16[320,5120]{1,0:T(8,128)(2,1)S(1)}, u32[]{:S(2)}) copy-start(bf16[320,5120]{1,0:T(8,128)(2,1)S(1)} %get-tuple-element.646) | copy-start | bytes 9830404
where the time goes:
time: 84.5 us; the launch traced here: 83.2 us
  Pallas kernels  32.2 us (38%)
  starting transfers between devices  29.9 us (35%)
  waiting for transfers between devices  17.7 us (21%)
  local copies, waits for them, and re-layouts  1.76 us (2%)
  between operations  1.33 us (2%)
    ppermute x12, starting transfers between devices, swap_pairs(): return lax.ppermute(block, 'frame', route)  20.7 us
    pallas_call x3, Pallas kernels, spatial_piece(): pl.pallas_call(functools.partial(spatial_kernel, math.log2(math.e) / math...  19.4 us
    ppermute x12, waiting for transfers between devices, swap_pairs(): return lax.ppermute(block, 'frame', route)  9.52 us
    ppermute x8, waiting for transfers between devices, swap_bit(): lax.ppermute(block, 'frame', [(i, i ^ 1 << bit) for i in range(count)])  7.9 us
    ppermute x8, starting transfers between devices, swap_bit(): lax.ppermute(block, 'frame', [(i, i ^ 1 << bit) for i in range(count)])  7.8 us
    pallas_call x3, Pallas kernels, temporal(): pl.pallas_call(functools.partial(temporal_kernel, math.log2(math.e) / mat...  6.55 us
    pallas_call x1, Pallas kernels, extract(): pl.pallas_call(functools.partial(extract_kernel, reach), out_shape=(jax.S...  3.44 us
    unnamed x4, local copies, waits for them, and re-layouts  1.71 us
  transfers between devices with their start and end apart: 21, of which 7 were waited for; matrix products, arithmetic and copies ran while one was open for 0% of the time, Pallas kernels for 38%

commit v1 on v0

--- a/solution.py
+++ b/solution.py
@@ -63,7 +63,7 @@
 
 def extract_kernel(
     reach, labels_hbm, band_hbm, keys, values,
-    meta, choice, pair_keep, high_send, low_send, labels, band, found, sems,
+    meta, choice, pair_keep, labels, band, found, sems,
 ):
     heads = labels.shape[0]
     half = pair_keep.shape[2]
@@ -83,7 +83,7 @@
         temporal = temporal + labels[head]
     listed_heads = [found[number] for number in range(TEMP_HEADS)]
     bands = [band[head] for head in listed_heads]
-    kept, sent = rows_of(side, half), rows_of(1 - side, half)
+    kept = rows_of(side, half)
     for number, head in enumerate(listed_heads):
         rank = jnp.int32(0)
         for other in range(TEMP_HEADS):
@@ -95,14 +95,6 @@
         columns = columns_of(head)
         for kind, source in enumerate((keys, values)):
             pltpu.make_async_copy(source.at[kept, columns], pair_keep.at[rank, kind], sems.at[2]).start()
-
-            @pl.when(rank < HIGH)
-            def _():
-                pltpu.make_async_copy(source.at[sent, columns], high_send.at[rank, kind], sems.at[3]).start()
-
-            @pl.when(rank >= HIGH)
-            def _():
-                pltpu.make_async_copy(source.at[sent, columns], low_send.at[rank - HIGH, kind], sems.at[4]).start()
 
     spatial = jnp.int32(0)
     for head in range(heads):
@@ -124,35 +116,63 @@
 
             listed = listed + is_needed.astype(jnp.int32)
     choice[0] = sum((listed > level).astype(jnp.int32) for level in LEVELS[:-1])
-    for number, whole in enumerate((pair_keep, high_send, low_send)):
-        pltpu.make_async_copy(whole, whole, sems.at[2 + number]).wait()
+    pltpu.make_async_copy(pair_keep, pair_keep, sems.at[2]).wait()
 
 
 def extract(reach, labels, band, keys, values):
     half = keys.shape[0] // 2
-    pair = [
-        jax.ShapeDtypeStruct((count, 2, half, HEAD_DIM), jnp.bfloat16)
-        for count in (TEMP_HEADS, HIGH, TEMP_HEADS - HIGH)
-    ]
+    pair = jax.ShapeDtypeStruct((TEMP_HEADS, 2, half, HEAD_DIM), jnp.bfloat16)
     return pl.pallas_call(
         functools.partial(extract_kernel, reach),
         out_shape=(
             jax.ShapeDtypeStruct((3 * labels.shape[0] + 4 * TEMP_HEADS,), jnp.int32),
             jax.ShapeDtypeStruct((1,), jnp.int32),
-            *pair,
+            pair,
         ),
         in_specs=[HBM] * 4,
-        out_specs=(SMEM, SMEM) + (VMEM,) * 3,
+        out_specs=(SMEM, SMEM, VMEM),
         scratch_shapes=[
             pltpu.SMEM(labels.shape, jnp.int32),
             pltpu.SMEM(band.shape, jnp.int32),
             pltpu.SMEM((TEMP_HEADS + 1,), jnp.int32),
-            pltpu.SemaphoreType.DMA((5,)),
+            pltpu.SemaphoreType.DMA((3,)),
         ],
         compiler_params=pltpu.CompilerParams(vmem_limit_bytes=58 * MIB),
         cost_estimate=pl.CostEstimate(flops=0, bytes_accessed=8 * TEMP_HEADS * half * HEAD_DIM * 2, transcendentals=0),
         name="extract_temporal",
     )(labels, band, keys, values)
+
+
+def sends_kernel(meta, keys, values, high_send, low_send, sems):
+    heads = (meta.shape[0] - 4 * TEMP_HEADS) // 3
+    half = high_send.shape[2]
+    side, _ = position()
+    sent = rows_of(1 - side, half)
+    for number in range(TEMP_HEADS):
+        columns = columns_of(meta[heads + number])
+        block = high_send.at[number] if number < HIGH else low_send.at[number - HIGH]
+        for kind, source in enumerate((keys, values)):
+            copy = pltpu.make_async_copy(source.at[sent, columns], block.at[kind], sems.at[0 if number < HIGH else 1])
+            copy.start()
+    for number, whole in enumerate((high_send, low_send)):
+        pltpu.make_async_copy(whole, whole, sems.at[number]).wait()
+
+
+def extract_sends(meta, keys, values):
+    half = keys.shape[0] // 2
+    outs = [
+        jax.ShapeDtypeStruct((count, 2, half, HEAD_DIM), jnp.bfloat16) for count in (HIGH, TEMP_HEADS - HIGH)
+    ]
+    return pl.pallas_call(
+        sends_kernel,
+        out_shape=tuple(outs),
+        in_specs=[SMEM, HBM, HBM],
+        out_specs=(VMEM, VMEM),
+        scratch_shapes=[pltpu.SemaphoreType.DMA((2,))],
+        compiler_params=pltpu.CompilerParams(vmem_limit_bytes=50 * MIB),
+        cost_estimate=pl.CostEstimate(flops=0, bytes_accessed=4 * TEMP_HEADS * half * HEAD_DIM * 2, transcendentals=0),
+        name="extract_sends",
+    )(meta, keys, values)
 
 
 def queries_kernel(meta, queries, query_keep, query_send, sems):
@@ -462,7 +482,8 @@
 
     keys_far = swap_bit(keys, 0)
     values_far = swap_bit(values, 0)
-    meta, choice, pair_keep, high_send, low_send = extract(reach, labels, band, keys, values)
+    meta, choice, pair_keep = extract(reach, labels, band, keys, values)
+    high_send, low_send = extract_sends(meta, keys, values)
 
     def attend_piece(result, number):
         first, count = sum(SPATIAL_PIECES[:number]), SPATIAL_PIECES[number]

time: 84.5 us -> 86.1 us (1.019); the launches traced: 83.2 us -> 87.1 us
  Pallas kernels: 32.2 us -> 35.9 us
  starting transfers between devices: 29.9 us -> 31.1 us
  waiting for transfers between devices: 17.7 us -> 16.6 us
    pallas_call x0 -> x1, Pallas kernels: none -> 1.86 us  [extract_sends(): pl.pallas_call(sends_kernel, out_shape=tuple(outs), in_specs=[SMEM, HBM,...]
    ppermute x12, waiting for transfers between devices: 9.52 us -> 7.78 us  [swap_pairs(): return lax.ppermute(block, 'frame', route)]
    pallas_call x3, Pallas kernels: 6.55 us -> 8.21 us  [temporal(): pl.pallas_call(functools.partial(temporal_kernel, math.log2(math.e) / mat...]
    ppermute x12, starting transfers between devices: 20.7 us -> 22.1 us  [swap_pairs(): return lax.ppermute(block, 'frame', route)]
  transfers between devices with their start and end apart: 21 -> 21, of which waited for: 7 -> 6; matrix products, arithmetic and copies ran while one was open for 0% -> 0% of each run, Pallas kernels for 38% -> 40%
where the time goes in v1:
time: 86.1 us; the launch traced here: 87.1 us
  Pallas kernels  35.9 us (42%)
  starting transfers between devices  31.1 us (36%)
  waiting for transfers between devices  16.6 us (19%)
  local copies, waits for them, and re-layouts  1.77 us (2%)
  between operations  1.44 us (2%)
    ppermute x12, starting transfers between devices, swap_pairs(): return lax.ppermute(block, 'frame', route)  22.1 us
    pallas_call x3, Pallas kernels, spatial_piece(): pl.pallas_call(functools.partial(spatial_kernel, math.log2(math.e) / math...  19.4 us
    ppermute x8, waiting for transfers between devices, swap_bit(): lax.ppermute(block, 'frame', [(i, i ^ 1 << bit) for i in range(count)])  8.62 us
    pallas_call x3, Pallas kernels, temporal(): pl.pallas_call(functools.partial(temporal_kernel, math.log2(math.e) / mat...  8.21 us
    ppermute x12, waiting for transfers between devices, swap_pairs(): return lax.ppermute(block, 'frame', route)  7.78 us
    ppermute x8, starting transfers between devices, swap_bit(): lax.ppermute(block, 'frame', [(i, i ^ 1 << bit) for i in range(count)])  7.51 us
    pallas_call x1, Pallas kernels, extract(): pl.pallas_call(functools.partial(extract_kernel, reach), out_shape=(jax.S...  3.12 us
    pallas_call x1, Pallas kernels, extract_sends(): pl.pallas_call(sends_kernel, out_shape=tuple(outs), in_specs=[SMEM, HBM,...  1.86 us
  transfers between devices with their start and end apart: 21, of which 6 were waited for; matrix products, arithmetic and copies ran while one was open for 0% of the time, Pallas kernels for 40%

profile of v1, /device:TPU:0, one launch (start us, length us, event | category | flops | bytes accessed | tf_op | source)
XLA Modules:
  0.0 87.1 jit_solution(6343291522969184164)
XLA Ops:
  0.0 0.5 collective-permute-start.47
  0.5 0.1 collective-permute-start.48
  0.5 3.1 %extract_temporal.1 = (s32[160]{0:T(256)S(1)}, s32[1]{0:T(128)}, bf16[10,2,160,128]{3,2,1,0:T(8,128)(2,1)}) custom-call(s32[40]{0:T(128)} %labels_hbm.1, s32[40]{0:T(128)} %band_hbm.1, bf16[320,5120]{1,0:T(8,128)(2,1)} %refs_11_.5, bf16[320,5120]{1,0:T(8,128)(2,1)} %refs_12_.5), custom_call_target="tpu_custom_call" | custom-call | bytes 3276800 | tf_op jit(solution)/shard_map/extract_temporal/pallas_call | solution.py:125
  3.6 0.7 collective-permute-start.44
  4.4 5.9 %collective-permute-start.43 = (bf16[10,2,160,128]{3,2,1,0:T(8,128)(2,1)}, bf16[10,2,160,128]{3,2,1,0:T(8,128)(2,1)S(1)}, u32[]{:S(2)}, u32[]{:S(2)}) collective-permute-start(bf16[10,2,160,128]{3,2,1,0:T(8,128)(2,1)} %get-tuple-element.533), channel_id=1, source_target_pairs={{0,4},{1,5},{2,6},{3,7},{4,0},{5,1},{6,2},{7,3},{8,12},{9,13},{10,... | collective-permute-start | bytes 2457608 | tf_op jit(solution)/shard_map/ppermute | solution.py:39
  10.2 1.9 %extract_sends.1 = (bf16[5,2,160,128]{3,2,1,0:T(8,128)(2,1)S(1)}, bf16[5,2,160,128]{3,2,1,0:T(8,128)(2,1)S(1)}) custom-call(s32[160]{0:T(256)S(1)} %get-tuple-element.537.meta, bf16[320,5120]{1,0:T(8,128)(2,1)S(1)} %copy-done, bf16[320,5120]{1,0:T(8,128)(2,1)} %refs_12_.5), custom_call_target="tpu_custom_call" | custom-call | bytes 1638400 | tf_op jit(solution)/shard_map/extract_sends/pallas_call | solution.py:166
  12.1 1.6 %collective-permute-start.46 = (bf16[5,2,160,128]{3,2,1,0:T(8,128)(2,1)S(1)}, bf16[5,2,160,128]{3,2,1,0:T(8,128)(2,1)S(1)}, u32[]{:S(2)}, u32[]{:S(2)}) collective-permute-start(bf16[5,2,160,128]{3,2,1,0:T(8,128)(2,1)S(1)} %get-tuple-element.536), channel_id=1, source_target_pairs={{0,2},{1,3},{2,0},{3,1},{4,6},{5,7},{6,4},{7,5},{8,10},{9,11},{10,... | collective-permute-start | bytes 1228808 | tf_op jit(solution)/shard_map/ppermute | solution.py:27
  13.7 0.5 collective-permute-start.45
  14.2 0.0 collective-permute-done.48.refs_4_.refs_9_.refs_14_
  14.2 6.0 %spatial_heads.3.refs_15_ = bf16[320,5120]{1,0:T(8,128)(2,1)S(1)} custom-call(s32[160]{0:T(256)S(1)} %get-tuple-element.537.meta, bf16[320,5120]{1,0:T(8,128)(2,1)S(1)} %copy-done.1, bf16[320,5120]{1,0:T(8,128)(2,1)} %refs_11_.5, bf16[320,5120]{1,0:T(8,128)(2,1)} %refs_12_.5, bf16[320,5120]{1,0:T(8,128)(2,1)} %collective-permute-done.47.refs_3_.refs_8_.refs_13_, ...), custom_call_target="tpu_custom_call" | custom-call | flops 943718400 | bytes 4423680 | tf_op jit(solution)/shard_map/spatial_heads/pallas_call | solution.py:264
  20.2 0.9 %extract_queries.1 = (bf16[10,160,128]{2,1,0:T(8,128)(2,1)S(1)}, bf16[10,160,128]{2,1,0:T(8,128)(2,1)S(1)}) custom-call(s32[160]{0:T(256)S(1)} %get-tuple-element.537.meta, bf16[320,5120]{1,0:T(8,128)(2,1)S(1)} %copy-done.1), custom_call_target="tpu_custom_call" | custom-call | bytes 1638400 | tf_op jit(solution)/shard_map/extract_queries/pallas_call | solution.py:194
  21.1 3.5 %collective-permute-done.46 = bf16[5,2,160,128]{3,2,1,0:T(8,128)(2,1)S(1)} collective-permute-done((bf16[5,2,160,128]{3,2,1,0:T(8,128)(2,1)S(1)}, bf16[5,2,160,128]{3,2,1,0:T(8,128)(2,1)S(1)}, u32[]{:S(2)}, u32[]{:S(2)}) %collective-permute-start.46) | collective-permute-done | bytes 409632 | tf_op jit(solution)/shard_map/ppermute | solution.py:27
  24.6 0.7 collective-permute-start.50
  25.2 1.7 %collective-permute-start.49 = (bf16[5,2,160,128]{3,2,1,0:T(8,128)(2,1)S(1)}, bf16[5,2,160,128]{3,2,1,0:T(8,128)(2,1)S(1)}, u32[]{:S(2)}, u32[]{:S(2)}) collective-permute-start(bf16[5,2,160,128]{3,2,1,0:T(8,128)(2,1)S(1)} %collective-permute-done.46), channel_id=1, source_target_pairs={{0,4},{1,5},{2,6},{3,7},{4,0},{5,1},{6,2},{7,3},{8,12},{9,13},{10,... | collective-permute-start | bytes 1228808 | tf_op jit(solution)/shard_map/ppermute | solution.py:39
  27.0 4.5 %spatial_heads.4.refs_15_ = bf16[320,5120]{1,0:T(8,128)(2,1)S(1)} custom-call(s32[160]{0:T(256)S(1)} %get-tuple-element.537.meta, bf16[320,5120]{1,0:T(8,128)(2,1)S(1)} %copy-done.1, bf16[320,5120]{1,0:T(8,128)(2,1)} %refs_11_.5, bf16[320,5120]{1,0:T(8,128)(2,1)} %refs_12_.5, ...), custom_call_target="tpu_custom_call", output_to_operand_aliasing={{}: (16, {})} | custom-call | flops 629145600 | bytes 2949120 | tf_op jit(solution)/shard_map/spatial_heads/pallas_call | solution.py:264
  31.5 0.3 collective-permute-done.45
  31.8 0.0 collective-permute-done.44
  31.8 0.0 collective-permute-done.43
  31.8 1.5 %collective-permute-start.56 = (s32[1]{0:T(128)}, s32[1]{0:T(128)}, u32[]{:S(2)}, u32[]{:S(2)}) collective-permute-start(s32[1]{0:T(128)} %get-tuple-element.551), channel_id=1, source_target_pairs={{0,16},{16,0},{1,17},{17,1},{2,18},{18,2},{3,19},{19,3},{4,20},{20... | collective-permute-start | bytes 20 | tf_op jit(solution)/shard_map/ppermute | solution.py:47
  33.4 1.3 %collective-permute-start.54 = (bf16[5,2,160,128]{3,2,1,0:T(8,128)(2,1)S(1)}, bf16[5,2,160,128]{3,2,1,0:T(8,128)(2,1)S(1)}, u32[]{:S(2)}, u32[]{:S(2)}) collective-permute-start(bf16[5,2,160,128]{3,2,1,0:T(8,128)(2,1)S(1)} %slice.7), channel_id=1, source_target_pairs={{4,0},{5,1},{6,2},{7,3},{8,12},{9,13},{10,14},{11,15},{20,16},{21,... | collective-permute-start | bytes 1228808 | tf_op jit(solution)/shard_map/ppermute | solution.py:39
  34.7 0.7 collective-permute-start.53
  35.4 0.2 collective-permute-done.56
  35.5 1.5 %collective-permute-start.55 = (bf16[10,160,128]{2,1,0:T(8,128)(2,1)S(1)}, bf16[10,160,128]{2,1,0:T(8,128)(2,1)S(1)}, u32[]{:S(2)}, u32[]{:S(2)}) collective-permute-start(bf16[10,160,128]{2,1,0:T(8,128)(2,1)S(1)} %get-tuple-element.550), channel_id=1, source_target_pairs={{0,2},{1,3},{2,0},{3,1},{4,6},{5,7},{6,4},{7,5},{8,10},{9,11},{10,... | collective-permute-start | bytes 1228808 | tf_op jit(solution)/shard_map/ppermute | solution.py:27
  37.0 0.0 collective-permute-done.50
  37.0 0.7 collective-permute-start.52
  37.7 0.6 collective-permute-done.49
  38.3 6.6 %collective-permute-start.51 = (bf16[5,2,160,128]{3,2,1,0:T(8,128)(2,1)S(1)}, bf16[5,2,160,128]{3,2,1,0:T(8,128)(2,1)S(1)}, u32[]{:S(2)}, u32[]{:S(2)}) collective-permute-start(bf16[5,2,160,128]{3,2,1,0:T(8,128)(2,1)S(1)} %collective-permute-done.45), channel_id=1, source_target_pairs={{0,4},{1,5},{2,6},{3,7},{4,0},{5,1},{6,2},{7,3},{8,12},{9,13},{10,... | collective-permute-start | bytes 1228808 | tf_op jit(solution)/shard_map/ppermute | solution.py:39
  46.1 8.9 %spatial_heads.5 = bf16[320,5120]{1,0:T(8,128)(2,1)S(1)} custom-call(s32[160]{0:T(256)S(1)} %get-tuple-element.537.meta, bf16[320,5120]{1,0:T(8,128)(2,1)S(1)} %copy-done.1, bf16[320,5120]{1,0:T(8,128)(2,1)} %refs_11_.5, bf16[320,5120]{1,0:T(8,128)(2,1)} %refs_12_.5, ...), custom_call_target="tpu_custom_call", output_to_operand_aliasing={{}: (16, {})} | custom-call | flops 1572864000 | bytes 7372800 | tf_op jit(solution)/shard_map/spatial_heads/pallas_call | solution.py:264
  55.0 0.0 collective-permute-done.54
  55.1 0.0 collective-permute-done.55
  55.1 0.0 collective-permute-done.52
  55.1 30.3 %conditional.1 = (bf16[320,5120]{1,0:T(8,128)(2,1)S(1)}) conditional(s32[]{:T(128)} %bitcast, (s32[160]{0:T(256)S(1)}, bf16[10,160,128]{2,1,0:T(8,128)(2,1)S(1)}, bf16[10,160,128]{2,1,0:T(8,128)(2,1)S(1)}, bf16[10,2,160,128]{3,2,1,0:T(8,128)(2,1)}, bf16[5,2,160,128]{3,2,1,0:T(8,128)(2,1)S(1)}, ...), branch_computations={%region_0.0_spmd, %region_1.0_spmd, %region_2.0_spmd, %region_3.0_... | conditional | flops 419430400 | bytes 20480248 | solution.py:544
  55.3 0.7 collective-permute-start.19
  56.0 1.3 %collective-permute-start.20 = (bf16[5,2,160,128]{3,2,1,0:T(8,128)(2,1)S(1)}, bf16[5,2,160,128]{3,2,1,0:T(8,128)(2,1)S(1)}, u32[]{:S(2)}, u32[]{:S(2)}) collective-permute-start(bf16[5,2,160,128]{3,2,1,0:T(8,128)(2,1)S(1)} %get-tuple-element.399.rest_5_), channel_id=1, source_target_pairs={{4,0},{5,1},{6,2},{7,3},{8,12},{9,13},{10,14},{11,15},{20,16},{21,... | collective-permute-start | bytes 1228808 | tf_op jit(solution)/shard_map/cond/branch_3_fun/ppermute | solution.py:39
  57.3 1.7 %temporal_heads.25 = (bf16[320,5120]{1,0:T(8,128)(2,1)S(1)}, bf16[1,160,128]{2,1,0:T(8,128)(2,1)S(1)}) custom-call(s32[160]{0:T(256)S(1)} %get-tuple-element.407.meta, bf16[10,160,128]{2,1,0:T(8,128)(2,1)S(1)} %get-tuple-element.406.query_own, bf16[10,160,128]{2,1,0:T(8,128)(2,1)S(1)} %get-tuple-element.387.query_far, ...), custom_call_target="tpu_custom_call", output_to_operand_aliasing={{0}: (9, {})} | custom-call | flops 41943040 | bytes 819200 | tf_op jit(solution)/shard_map/cond/branch_3_fun/temporal_heads/pallas_call | solution.py:431
  59.0 1.6 %pack_items.8 = (bf16[4,2,160,128]{3,2,1,0:T(8,128)(2,1)S(1)}, bf16[4,2,160,128]{3,2,1,0:T(8,128)(2,1)S(1)}) custom-call(s32[160]{0:T(256)S(1)} %get-tuple-element.407.meta, bf16[10,2,160,128]{3,2,1,0:T(8,128)(2,1)S(1)} %get-tuple-element.408.own_a, bf16[5,2,160,128]{3,2,1,0:T(8,128)(2,1)S(1)} %get-tuple-element.409.low_a, ...), custom_call_target="tpu_custom_call" | custom-call | tf_op jit(solution)/shard_map/cond/branch_3_fun/pack_items/pallas_call | solution.py:321
  60.6 1.3 %collective-permute-start.22 = (bf16[4,2,160,128]{3,2,1,0:T(8,128)(2,1)S(1)}, bf16[4,2,160,128]{3,2,1,0:T(8,128)(2,1)S(1)}, u32[]{:S(2)}, u32[]{:S(2)}) collective-permute-start(bf16[4,2,160,128]{3,2,1,0:T(8,128)(2,1)S(1)} %get-tuple-element.412), channel_id=1, source_target_pairs={{4,0},{5,1},{6,2},{7,3},{8,12},{9,13},{10,14},{11,15},{20,16},{21,... | collective-permute-start | bytes 983048 | tf_op jit(solution)/shard_map/cond/branch_3_fun/ppermute | solution.py:39
  61.9 0.7 collective-permute-start.23
  62.6 1.2 %collective-permute-start.18 = (bf16[1,160,128]{2,1,0:T(8,128)(2,1)S(1)}, bf16[1,160,128]{2,1,0:T(8,128)(2,1)S(1)}, u32[]{:S(2)}, u32[]{:S(2)}) collective-permute-start(bf16[1,160,128]{2,1,0:T(8,128)(2,1)S(1)} %get-tuple-element.395), channel_id=1, source_target_pairs={{0,2},{1,3},{2,0},{3,1},{4,6},{5,7},{6,4},{7,5},{8,10},{9,11},{10,... | collective-permute-start | bytes 122888 | tf_op jit(solution)/shard_map/cond/branch_3_fun/ppermute | solution.py:27
  63.8 7.2 %collective-permute-done.20.rest_9_ = bf16[5,2,160,128]{3,2,1,0:T(8,128)(2,1)S(1)} collective-permute-done((bf16[5,2,160,128]{3,2,1,0:T(8,128)(2,1)S(1)}, bf16[5,2,160,128]{3,2,1,0:T(8,128)(2,1)S(1)}, u32[]{:S(2)}, u32[]{:S(2)}) %collective-permute-start.20) | collective-permute-done | bytes 409632 | tf_op jit(solution)/shard_map/cond/branch_3_fun/ppermute | solution.py:39
  71.0 3.5 %temporal_heads.26 = (bf16[5,160,128]{2,1,0:T(8,128)(2,1)S(1)}, bf16[5,160,128]{2,1,0:T(8,128)(2,1)S(1)}) custom-call(s32[160]{0:T(256)S(1)} %get-tuple-element.407.meta, bf16[10,160,128]{2,1,0:T(8,128)(2,1)S(1)} %get-tuple-element.406.query_own, bf16[10,160,128]{2,1,0:T(8,128)(2,1)S(1)} %get-tuple-element.387.query_far, ...), custom_call_target="tpu_custom_call" | custom-call | flops 209715200 | bytes 4096000 | tf_op jit(solution)/shard_map/cond/branch_3_fun/temporal_heads/pallas_call | solution.py:431
  74.5 1.6 %collective-permute-start.21 = (bf16[5,160,128]{2,1,0:T(8,128)(2,1)S(1)}, bf16[5,160,128]{2,1,0:T(8,128)(2,1)S(1)}, u32[]{:S(2)}, u32[]{:S(2)}) collective-permute-start(bf16[5,160,128]{2,1,0:T(8,128)(2,1)S(1)} %get-tuple-element.405), channel_id=1, source_target_pairs={{0,2},{1,3},{2,0},{3,1},{4,6},{5,7},{6,4},{7,5},{8,10},{9,11},{10,... | collective-permute-start | bytes 614408 | tf_op jit(solution)/shard_map/cond/branch_3_fun/ppermute | solution.py:27
  76.1 3.0 %temporal_heads.27 = (bf16[4,160,128]{2,1,0:T(8,128)(2,1)S(1)}, bf16[4,160,128]{2,1,0:T(8,128)(2,1)S(1)}) custom-call(s32[160]{0:T(256)S(1)} %get-tuple-element.407.meta, bf16[10,160,128]{2,1,0:T(8,128)(2,1)S(1)} %get-tuple-element.406.query_own, bf16[10,160,128]{2,1,0:T(8,128)(2,1)S(1)} %get-tuple-element.387.query_far, ...), custom_call_target="tpu_custom_call" | custom-call | flops 167772160 | bytes 3276800 | tf_op jit(solution)/shard_map/cond/branch_3_fun/temporal_heads/pallas_call | solution.py:431
  79.2 0.6 collective-permute-start.24
  79.7 4.8 %collective-permute-done.24.refs_4_ = bf16[4,160,128]{2,1,0:T(8,128)(2,1)S(1)} collective-permute-done((bf16[4,160,128]{2,1,0:T(8,128)(2,1)S(1)}, bf16[4,160,128]{2,1,0:T(8,128)(2,1)S(1)}, u32[]{:S(2)}, u32[]{:S(2)}) %collective-permute-start.24) | collective-permute-done | bytes 163872 | tf_op jit(solution)/shard_map/cond/branch_3_fun/ppermute | solution.py:27
  84.6 0.8 finish.10
  85.4 0.0 copy-start.2
  85.4 1.7 %copy-done.2 = bf16[320,5120]{1,0:T(8,128)(2,1)} copy-done((bf16[320,5120]{1,0:T(8,128)(2,1)}, bf16[320,5120]{1,0:T(8,128)(2,1)S(1)}, u32[]{:S(2)}) %copy-start.2) | copy-done | bytes 3276824
  (14 shorter events, 0.1 us)
Async XLA Ops:
  0.0 10.2 %copy-start = (bf16[320,5120]{1,0:T(8,128)(2,1)S(1)}, bf16[320,5120]{1,0:T(8,128)(2,1)}, u32[]{:S(2)}) copy-start(bf16[320,5120]{1,0:T(8,128)(2,1)} %refs_11_.5) | copy-start | bytes 9830404
  0.0 13.7 %collective-permute-start.47 = (bf16[320,5120]{1,0:T(8,128)(2,1)}, bf16[320,5120]{1,0:T(8,128)(2,1)}, u32[]{:S(2)}, u32[]{:S(2)}) collective-permute-start(bf16[320,5120]{1,0:T(8,128)(2,1)} %refs_11_.5), channel_id=1, source_target_pairs={{0,1},{1,0},{2,3},{3,2},{4,5},{5,4},{6,7},{7,6},{8,9},{9,8},{10,11... | collective-permute-start | bytes 9830408 | tf_op jit(solution)/shard_map/ppermute | solution.py:27
  0.5 13.7 %collective-permute-start.48 = (bf16[320,5120]{1,0:T(8,128)(2,1)}, bf16[320,5120]{1,0:T(8,128)(2,1)}, u32[]{:S(2)}, u32[]{:S(2)}) collective-permute-start(bf16[320,5120]{1,0:T(8,128)(2,1)} %refs_12_.5), channel_id=1, source_target_pairs={{0,1},{1,0},{2,3},{3,2},{4,5},{5,4},{6,7},{7,6},{8,9},{9,8},{10,11... | collective-permute-start | bytes 9830408 | tf_op jit(solution)/shard_map/ppermute | solution.py:27
  3.6 28.2 %collective-permute-start.44 = (bf16[10,2,160,128]{3,2,1,0:T(8,128)(2,1)}, bf16[10,2,160,128]{3,2,1,0:T(8,128)(2,1)S(1)}, u32[]{:S(2)}, u32[]{:S(2)}) collective-permute-start(bf16[10,2,160,128]{3,2,1,0:T(8,128)(2,1)} %get-tuple-element.533), channel_id=1, source_target_pairs={{4,8},{5,9},{6,10},{7,11},{8,4},{9,5},{10,6},{11,7},{20,24},{21,25... | collective-permute-start | bytes 2457608 | tf_op jit(solution)/shard_map/ppermute | solution.py:39
  4.4 27.4 %collective-permute-start.43 = (bf16[10,2,160,128]{3,2,1,0:T(8,128)(2,1)}, bf16[10,2,160,128]{3,2,1,0:T(8,128)(2,1)S(1)}, u32[]{:S(2)}, u32[]{:S(2)}) collective-permute-start(bf16[10,2,160,128]{3,2,1,0:T(8,128)(2,1)} %get-tuple-element.533), channel_id=1, source_target_pairs={{0,4},{1,5},{2,6},{3,7},{4,0},{5,1},{6,2},{7,3},{8,12},{9,13},{10,... | collective-permute-start | bytes 2457608 | tf_op jit(solution)/shard_map/ppermute | solution.py:39
  10.2 4.0 %copy-start.1 = (bf16[320,5120]{1,0:T(8,128)(2,1)S(1)}, bf16[320,5120]{1,0:T(8,128)(2,1)}, u32[]{:S(2)}) copy-start(bf16[320,5120]{1,0:T(8,128)(2,1)} %refs_10_.5) | copy-start | bytes 9830404
  12.1 12.5 %collective-permute-start.46 = (bf16[5,2,160,128]{3,2,1,0:T(8,128)(2,1)S(1)}, bf16[5,2,160,128]{3,2,1,0:T(8,128)(2,1)S(1)}, u32[]{:S(2)}, u32[]{:S(2)}) collective-permute-start(bf16[5,2,160,128]{3,2,1,0:T(8,128)(2,1)S(1)} %get-tuple-element.536), channel_id=1, source_target_pairs={{0,2},{1,3},{2,0},{3,1},{4,6},{5,7},{6,4},{7,5},{8,10},{9,11},{10,... | collective-permute-start | bytes 1228808 | tf_op jit(solution)/shard_map/ppermute | solution.py:27
  13.7 18.1 %collective-permute-start.45 = (bf16[5,2,160,128]{3,2,1,0:T(8,128)(2,1)S(1)}, bf16[5,2,160,128]{3,2,1,0:T(8,128)(2,1)S(1)}, u32[]{:S(2)}, u32[]{:S(2)}) collective-permute-start(bf16[5,2,160,128]{3,2,1,0:T(8,128)(2,1)S(1)} %get-tuple-element.535), channel_id=1, source_target_pairs={{0,2},{1,3},{2,0},{3,1},{4,6},{5,7},{6,4},{7,5},{8,10},{9,11},{10,... | collective-permute-start | bytes 1228808 | tf_op jit(solution)/shard_map/ppermute | solution.py:27
  24.6 12.5 %collective-permute-start.50 = (bf16[5,2,160,128]{3,2,1,0:T(8,128)(2,1)S(1)}, bf16[5,2,160,128]{3,2,1,0:T(8,128)(2,1)S(1)}, u32[]{:S(2)}, u32[]{:S(2)}) collective-permute-start(bf16[5,2,160,128]{3,2,1,0:T(8,128)(2,1)S(1)} %collective-permute-done.46), channel_id=1, source_target_pairs={{4,8},{5,9},{6,10},{7,11},{8,4},{9,5},{10,6},{11,7},{20,24},{21,25... | collective-permute-start | bytes 1228808 | tf_op jit(solution)/shard_map/ppermute | solution.py:39
  25.2 13.0 %collective-permute-start.49 = (bf16[5,2,160,128]{3,2,1,0:T(8,128)(2,1)S(1)}, bf16[5,2,160,128]{3,2,1,0:T(8,128)(2,1)S(1)}, u32[]{:S(2)}, u32[]{:S(2)}) collective-permute-start(bf16[5,2,160,128]{3,2,1,0:T(8,128)(2,1)S(1)} %collective-permute-done.46), channel_id=1, source_target_pairs={{0,4},{1,5},{2,6},{3,7},{4,0},{5,1},{6,2},{7,3},{8,12},{9,13},{10,... | collective-permute-start | bytes 1228808 | tf_op jit(solution)/shard_map/ppermute | solution.py:39
  31.8 3.7 %collective-permute-start.56 = (s32[1]{0:T(128)}, s32[1]{0:T(128)}, u32[]{:S(2)}, u32[]{:S(2)}) collective-permute-start(s32[1]{0:T(128)} %get-tuple-element.551), channel_id=1, source_target_pairs={{0,16},{16,0},{1,17},{17,1},{2,18},{18,2},{3,19},{19,3},{4,20},{20... | collective-permute-start | bytes 20 | tf_op jit(solution)/shard_map/ppermute | solution.py:47
  33.4 21.7 %collective-permute-start.54 = (bf16[5,2,160,128]{3,2,1,0:T(8,128)(2,1)S(1)}, bf16[5,2,160,128]{3,2,1,0:T(8,128)(2,1)S(1)}, u32[]{:S(2)}, u32[]{:S(2)}) collective-permute-start(bf16[5,2,160,128]{3,2,1,0:T(8,128)(2,1)S(1)} %slice.7), channel_id=1, source_target_pairs={{4,0},{5,1},{6,2},{7,3},{8,12},{9,13},{10,14},{11,15},{20,16},{21,... | collective-permute-start | bytes 1228808 | tf_op jit(solution)/shard_map/ppermute | solution.py:39
  34.7 20.4 %collective-permute-start.53 = (bf16[5,2,160,128]{3,2,1,0:T(8,128)(2,1)S(1)}, bf16[5,2,160,128]{3,2,1,0:T(8,128)(2,1)S(1)}, u32[]{:S(2)}, u32[]{:S(2)}) collective-permute-start(bf16[5,2,160,128]{3,2,1,0:T(8,128)(2,1)S(1)} %slice.6), channel_id=1, source_target_pairs={{4,8},{5,9},{6,10},{7,11},{8,4},{9,5},{10,6},{11,7},{20,24},{21,25... | collective-permute-start | bytes 1228808 | tf_op jit(solution)/shard_map/ppermute | solution.py:39
  35.5 19.5 %collective-permute-start.55 = (bf16[10,160,128]{2,1,0:T(8,128)(2,1)S(1)}, bf16[10,160,128]{2,1,0:T(8,128)(2,1)S(1)}, u32[]{:S(2)}, u32[]{:S(2)}) collective-permute-start(bf16[10,160,128]{2,1,0:T(8,128)(2,1)S(1)} %get-tuple-element.550), channel_id=1, source_target_pairs={{0,2},{1,3},{2,0},{3,1},{4,6},{5,7},{6,4},{7,5},{8,10},{9,11},{10,... | collective-permute-start | bytes 1228808 | tf_op jit(solution)/shard_map/ppermute | solution.py:27
  37.0 18.0 %collective-permute-start.52 = (bf16[5,2,160,128]{3,2,1,0:T(8,128)(2,1)S(1)}, bf16[5,2,160,128]{3,2,1,0:T(8,128)(2,1)S(1)}, u32[]{:S(2)}, u32[]{:S(2)}) collective-permute-start(bf16[5,2,160,128]{3,2,1,0:T(8,128)(2,1)S(1)} %collective-permute-done.45), channel_id=1, source_target_pairs={{4,8},{5,9},{6,10},{7,11},{8,4},{9,5},{10,6},{11,7},{20,24},{21,25... | collective-permute-start | bytes 1228808 | tf_op jit(solution)/shard_map/ppermute | solution.py:39
  38.3 16.8 %collective-permute-start.51 = (bf16[5,2,160,128]{3,2,1,0:T(8,128)(2,1)S(1)}, bf16[5,2,160,128]{3,2,1,0:T(8,128)(2,1)S(1)}, u32[]{:S(2)}, u32[]{:S(2)}) collective-permute-start(bf16[5,2,160,128]{3,2,1,0:T(8,128)(2,1)S(1)} %collective-permute-done.45), channel_id=1, source_target_pairs={{0,4},{1,5},{2,6},{3,7},{4,0},{5,1},{6,2},{7,3},{8,12},{9,13},{10,... | collective-permute-start | bytes 1228808 | tf_op jit(solution)/shard_map/ppermute | solution.py:39
  55.3 8.5 %collective-permute-start.19 = (bf16[5,2,160,128]{3,2,1,0:T(8,128)(2,1)S(1)}, bf16[5,2,160,128]{3,2,1,0:T(8,128)(2,1)S(1)}, u32[]{:S(2)}, u32[]{:S(2)}) collective-permute-start(bf16[5,2,160,128]{3,2,1,0:T(8,128)(2,1)S(1)} %get-tuple-element.398.rest_3_), channel_id=1, source_target_pairs={{4,8},{5,9},{6,10},{7,11},{8,4},{9,5},{10,6},{11,7},{20,24},{21,25... | collective-permute-start | bytes 1228808 | tf_op jit(solution)/shard_map/cond/branch_3_fun/ppermute | solution.py:39
  56.0 15.0 %collective-permute-start.20 = (bf16[5,2,160,128]{3,2,1,0:T(8,128)(2,1)S(1)}, bf16[5,2,160,128]{3,2,1,0:T(8,128)(2,1)S(1)}, u32[]{:S(2)}, u32[]{:S(2)}) collective-permute-start(bf16[5,2,160,128]{3,2,1,0:T(8,128)(2,1)S(1)} %get-tuple-element.399.rest_5_), channel_id=1, source_target_pairs={{4,0},{5,1},{6,2},{7,3},{8,12},{9,13},{10,14},{11,15},{20,16},{21,... | collective-permute-start | bytes 1228808 | tf_op jit(solution)/shard_map/cond/branch_3_fun/ppermute | solution.py:39
  60.6 15.5 %collective-permute-start.22 = (bf16[4,2,160,128]{3,2,1,0:T(8,128)(2,1)S(1)}, bf16[4,2,160,128]{3,2,1,0:T(8,128)(2,1)S(1)}, u32[]{:S(2)}, u32[]{:S(2)}) collective-permute-start(bf16[4,2,160,128]{3,2,1,0:T(8,128)(2,1)S(1)} %get-tuple-element.412), channel_id=1, source_target_pairs={{4,0},{5,1},{6,2},{7,3},{8,12},{9,13},{10,14},{11,15},{20,16},{21,... | collective-permute-start | bytes 983048 | tf_op jit(solution)/shard_map/cond/branch_3_fun/ppermute | solution.py:39
  61.9 14.2 %collective-permute-start.23 = (bf16[4,2,160,128]{3,2,1,0:T(8,128)(2,1)S(1)}, bf16[4,2,160,128]{3,2,1,0:T(8,128)(2,1)S(1)}, u32[]{:S(2)}, u32[]{:S(2)}) collective-permute-start(bf16[4,2,160,128]{3,2,1,0:T(8,128)(2,1)S(1)} %get-tuple-element.413), channel_id=1, source_target_pairs={{4,8},{5,9},{6,10},{7,11},{8,4},{9,5},{10,6},{11,7},{20,24},{21,25... | collective-permute-start | bytes 983048 | tf_op jit(solution)/shard_map/cond/branch_3_fun/ppermute | solution.py:39
  62.6 13.5 %collective-permute-start.18 = (bf16[1,160,128]{2,1,0:T(8,128)(2,1)S(1)}, bf16[1,160,128]{2,1,0:T(8,128)(2,1)S(1)}, u32[]{:S(2)}, u32[]{:S(2)}) collective-permute-start(bf16[1,160,128]{2,1,0:T(8,128)(2,1)S(1)} %get-tuple-element.395), channel_id=1, source_target_pairs={{0,2},{1,3},{2,0},{3,1},{4,6},{5,7},{6,4},{7,5},{8,10},{9,11},{10,... | collective-permute-start | bytes 122888 | tf_op jit(solution)/shard_map/cond/branch_3_fun/ppermute | solution.py:27
  74.5 10.0 %collective-permute-start.21 = (bf16[5,160,128]{2,1,0:T(8,128)(2,1)S(1)}, bf16[5,160,128]{2,1,0:T(8,128)(2,1)S(1)}, u32[]{:S(2)}, u32[]{:S(2)}) collective-permute-start(bf16[5,160,128]{2,1,0:T(8,128)(2,1)S(1)} %get-tuple-element.405), channel_id=1, source_target_pairs={{0,2},{1,3},{2,0},{3,1},{4,6},{5,7},{6,4},{7,5},{8,10},{9,11},{10,... | collective-permute-start | bytes 614408 | tf_op jit(solution)/shard_map/cond/branch_3_fun/ppermute | solution.py:27
  79.2 5.4 %collective-permute-start.24 = (bf16[4,160,128]{2,1,0:T(8,128)(2,1)S(1)}, bf16[4,160,128]{2,1,0:T(8,128)(2,1)S(1)}, u32[]{:S(2)}, u32[]{:S(2)}) collective-permute-start(bf16[4,160,128]{2,1,0:T(8,128)(2,1)S(1)} %get-tuple-element.415), channel_id=1, source_target_pairs={{0,2},{1,3},{2,0},{3,1},{4,6},{5,7},{6,4},{7,5},{8,10},{9,11},{10,... | collective-permute-start | bytes 491528 | tf_op jit(solution)/shard_map/cond/branch_3_fun/ppermute | solution.py:27
  85.4 1.7 %copy-start.2 = (bf16[320,5120]{1,0:T(8,128)(2,1)}, bf16[320,5120]{1,0:T(8,128)(2,1)S(1)}, u32[]{:S(2)}) copy-start(bf16[320,5120]{1,0:T(8,128)(2,1)S(1)} %get-tuple-element.649) | copy-start | bytes 9830404

commit v2 on v1

--- a/solution.py
+++ b/solution.py
@@ -11,7 +11,7 @@
 TEMP_HEADS = 10
 HEAD_DIM = 128
 PIXEL_BLOCK = 32
-SPATIAL_PIECES = (9, 6, 15)
+SPATIAL_PIECES = (12, 3, 15)
 STEP_HEADS = 3
 HIGH = 5
 LEVELS = (0, 2, 3, 4, 5, 6, 2 * (TEMP_HEADS - HIGH))

time: 86.1 us -> 86.3 us (level)
  no operation moved by 1% of the time
where the time goes in v2:
time: 86.3 us; the launch traced here: 87.5 us
  Pallas kernels  35.9 us (42%)
  starting transfers between devices  31.3 us (36%)
  waiting for transfers between devices  16.6 us (19%)
  local copies, waits for them, and re-layouts  1.77 us (2%)
  between operations  1.44 us (2%)
    ppermute x12, starting transfers between devices, swap_pairs(): return lax.ppermute(block, 'frame', route)  22.1 us
    pallas_call x3, Pallas kernels, spatial_piece(): pl.pallas_call(functools.partial(spatial_kernel, math.log2(math.e) / math...  19.4 us
    ppermute x8, waiting for transfers between devices, swap_bit(): lax.ppermute(block, 'frame', [(i, i ^ 1 << bit) for i in range(count)])  8.65 us
    pallas_call x3, Pallas kernels, temporal(): pl.pallas_call(functools.partial(temporal_kernel, math.log2(math.e) / mat...  8.21 us
    ppermute x12, waiting for transfers between devices, swap_pairs(): return lax.ppermute(block, 'frame', route)  7.8 us
    ppermute x8, starting transfers between devices, swap_bit(): lax.ppermute(block, 'frame', [(i, i ^ 1 << bit) for i in range(count)])  7.68 us
    pallas_call x1, Pallas kernels, extract(): pl.pallas_call(functools.partial(extract_kernel, reach), out_shape=(jax.S...  3.12 us
    pallas_call x1, Pallas kernels, extract_sends(): pl.pallas_call(sends_kernel, out_shape=tuple(outs), in_specs=[SMEM, HBM,...  1.86 us
  transfers between devices with their start and end apart: 21, of which 6 were waited for; matrix products, arithmetic and copies ran while one was open for 0% of the time, Pallas kernels for 40%

profile of v2, /device:TPU:0, one launch (start us, length us, event | category | flops | bytes accessed | tf_op | source)
XLA Modules:
  0.0 87.5 jit_solution(7178807656280850886)
XLA Ops:
  0.0 0.5 collective-permute-start.47
  0.5 0.1 collective-permute-start.48
  0.5 3.1 %extract_temporal.1 = (s32[160]{0:T(256)S(1)}, s32[1]{0:T(128)}, bf16[10,2,160,128]{3,2,1,0:T(8,128)(2,1)}) custom-call(s32[40]{0:T(128)} %labels_hbm.1, s32[40]{0:T(128)} %band_hbm.1, bf16[320,5120]{1,0:T(8,128)(2,1)} %refs_11_.5, bf16[320,5120]{1,0:T(8,128)(2,1)} %refs_12_.5), custom_call_target="tpu_custom_call" | custom-call | bytes 3276800 | tf_op jit(solution)/shard_map/extract_temporal/pallas_call | solution.py:125
  3.7 0.7 collective-permute-start.44
  4.4 5.9 %collective-permute-start.43 = (bf16[10,2,160,128]{3,2,1,0:T(8,128)(2,1)}, bf16[10,2,160,128]{3,2,1,0:T(8,128)(2,1)S(1)}, u32[]{:S(2)}, u32[]{:S(2)}) collective-permute-start(bf16[10,2,160,128]{3,2,1,0:T(8,128)(2,1)} %get-tuple-element.533), channel_id=1, source_target_pairs={{0,4},{1,5},{2,6},{3,7},{4,0},{5,1},{6,2},{7,3},{8,12},{9,13},{10,... | collective-permute-start | bytes 2457608 | tf_op jit(solution)/shard_map/ppermute | solution.py:39
  10.2 1.9 %extract_sends.1 = (bf16[5,2,160,128]{3,2,1,0:T(8,128)(2,1)S(1)}, bf16[5,2,160,128]{3,2,1,0:T(8,128)(2,1)S(1)}) custom-call(s32[160]{0:T(256)S(1)} %get-tuple-element.537.meta, bf16[320,5120]{1,0:T(8,128)(2,1)S(1)} %copy-done, bf16[320,5120]{1,0:T(8,128)(2,1)} %refs_12_.5), custom_call_target="tpu_custom_call" | custom-call | bytes 1638400 | tf_op jit(solution)/shard_map/extract_sends/pallas_call | solution.py:166
  12.1 1.6 %collective-permute-start.46 = (bf16[5,2,160,128]{3,2,1,0:T(8,128)(2,1)S(1)}, bf16[5,2,160,128]{3,2,1,0:T(8,128)(2,1)S(1)}, u32[]{:S(2)}, u32[]{:S(2)}) collective-permute-start(bf16[5,2,160,128]{3,2,1,0:T(8,128)(2,1)S(1)} %get-tuple-element.536), channel_id=1, source_target_pairs={{0,2},{1,3},{2,0},{3,1},{4,6},{5,7},{6,4},{7,5},{8,10},{9,11},{10,... | collective-permute-start | bytes 1228808 | tf_op jit(solution)/shard_map/ppermute | solution.py:27
  13.7 0.0 collective-permute-done.47.refs_3_.refs_8_.refs_13_
  13.7 0.5 collective-permute-start.45
  14.2 7.4 %spatial_heads.3.refs_15_ = bf16[320,5120]{1,0:T(8,128)(2,1)S(1)} custom-call(s32[160]{0:T(256)S(1)} %get-tuple-element.537.meta, bf16[320,5120]{1,0:T(8,128)(2,1)S(1)} %copy-done.1, bf16[320,5120]{1,0:T(8,128)(2,1)} %refs_11_.5, bf16[320,5120]{1,0:T(8,128)(2,1)} %refs_12_.5, bf16[320,5120]{1,0:T(8,128)(2,1)} %collective-permute-done.47.refs_3_.refs_8_.refs_13_, ...), custom_call_target="tpu_custom_call" | custom-call | flops 1258291200 | bytes 5898240 | tf_op jit(solution)/shard_map/spatial_heads/pallas_call | solution.py:264
  21.6 0.9 %extract_queries.1 = (bf16[10,160,128]{2,1,0:T(8,128)(2,1)S(1)}, bf16[10,160,128]{2,1,0:T(8,128)(2,1)S(1)}) custom-call(s32[160]{0:T(256)S(1)} %get-tuple-element.537.meta, bf16[320,5120]{1,0:T(8,128)(2,1)S(1)} %copy-done.1), custom_call_target="tpu_custom_call" | custom-call | bytes 1638400 | tf_op jit(solution)/shard_map/extract_queries/pallas_call | solution.py:194
  22.5 2.0 %collective-permute-done.46 = bf16[5,2,160,128]{3,2,1,0:T(8,128)(2,1)S(1)} collective-permute-done((bf16[5,2,160,128]{3,2,1,0:T(8,128)(2,1)S(1)}, bf16[5,2,160,128]{3,2,1,0:T(8,128)(2,1)S(1)}, u32[]{:S(2)}, u32[]{:S(2)}) %collective-permute-start.46) | collective-permute-done | bytes 409632 | tf_op jit(solution)/shard_map/ppermute | solution.py:27
  24.6 0.7 collective-permute-start.50
  25.2 1.7 %collective-permute-start.49 = (bf16[5,2,160,128]{3,2,1,0:T(8,128)(2,1)S(1)}, bf16[5,2,160,128]{3,2,1,0:T(8,128)(2,1)S(1)}, u32[]{:S(2)}, u32[]{:S(2)}) collective-permute-start(bf16[5,2,160,128]{3,2,1,0:T(8,128)(2,1)S(1)} %collective-permute-done.46), channel_id=1, source_target_pairs={{0,4},{1,5},{2,6},{3,7},{4,0},{5,1},{6,2},{7,3},{8,12},{9,13},{10,... | collective-permute-start | bytes 1228808 | tf_op jit(solution)/shard_map/ppermute | solution.py:39
  27.0 3.0 %spatial_heads.4.refs_15_ = bf16[320,5120]{1,0:T(8,128)(2,1)S(1)} custom-call(s32[160]{0:T(256)S(1)} %get-tuple-element.537.meta, bf16[320,5120]{1,0:T(8,128)(2,1)S(1)} %copy-done.1, bf16[320,5120]{1,0:T(8,128)(2,1)} %refs_11_.5, bf16[320,5120]{1,0:T(8,128)(2,1)} %refs_12_.5, ...), custom_call_target="tpu_custom_call", output_to_operand_aliasing={{}: (16, {})} | custom-call | flops 314572800 | bytes 1474560 | tf_op jit(solution)/shard_map/spatial_heads/pallas_call | solution.py:264
  30.0 1.8 %collective-permute-done.45 = bf16[5,2,160,128]{3,2,1,0:T(8,128)(2,1)S(1)} collective-permute-done((bf16[5,2,160,128]{3,2,1,0:T(8,128)(2,1)S(1)}, bf16[5,2,160,128]{3,2,1,0:T(8,128)(2,1)S(1)}, u32[]{:S(2)}, u32[]{:S(2)}) %collective-permute-start.45) | collective-permute-done | bytes 409632 | tf_op jit(solution)/shard_map/ppermute | solution.py:27
  31.8 1.5 %collective-permute-start.56 = (s32[1]{0:T(128)}, s32[1]{0:T(128)}, u32[]{:S(2)}, u32[]{:S(2)}) collective-permute-start(s32[1]{0:T(128)} %get-tuple-element.551), channel_id=1, source_target_pairs={{0,16},{16,0},{1,17},{17,1},{2,18},{18,2},{3,19},{19,3},{4,20},{20... | collective-permute-start | bytes 20 | tf_op jit(solution)/shard_map/ppermute | solution.py:47
  33.4 1.3 %collective-permute-start.54 = (bf16[5,2,160,128]{3,2,1,0:T(8,128)(2,1)S(1)}, bf16[5,2,160,128]{3,2,1,0:T(8,128)(2,1)S(1)}, u32[]{:S(2)}, u32[]{:S(2)}) collective-permute-start(bf16[5,2,160,128]{3,2,1,0:T(8,128)(2,1)S(1)} %slice.7), channel_id=1, source_target_pairs={{4,0},{5,1},{6,2},{7,3},{8,12},{9,13},{10,14},{11,15},{20,16},{21,... | collective-permute-start | bytes 1228808 | tf_op jit(solution)/shard_map/ppermute | solution.py:39
  34.7 0.7 collective-permute-start.53
  35.4 0.2 collective-permute-done.56
  35.5 1.5 %collective-permute-start.55 = (bf16[10,160,128]{2,1,0:T(8,128)(2,1)S(1)}, bf16[10,160,128]{2,1,0:T(8,128)(2,1)S(1)}, u32[]{:S(2)}, u32[]{:S(2)}) collective-permute-start(bf16[10,160,128]{2,1,0:T(8,128)(2,1)S(1)} %get-tuple-element.550), channel_id=1, source_target_pairs={{0,2},{1,3},{2,0},{3,1},{4,6},{5,7},{6,4},{7,5},{8,10},{9,11},{10,... | collective-permute-start | bytes 1228808 | tf_op jit(solution)/shard_map/ppermute | solution.py:27
  37.0 0.0 collective-permute-done.50
  37.0 0.7 collective-permute-start.52
  37.7 0.6 collective-permute-done.49
  38.3 6.6 %collective-permute-start.51 = (bf16[5,2,160,128]{3,2,1,0:T(8,128)(2,1)S(1)}, bf16[5,2,160,128]{3,2,1,0:T(8,128)(2,1)S(1)}, u32[]{:S(2)}, u32[]{:S(2)}) collective-permute-start(bf16[5,2,160,128]{3,2,1,0:T(8,128)(2,1)S(1)} %collective-permute-done.45), channel_id=1, source_target_pairs={{0,4},{1,5},{2,6},{3,7},{4,0},{5,1},{6,2},{7,3},{8,12},{9,13},{10,... | collective-permute-start | bytes 1228808 | tf_op jit(solution)/shard_map/ppermute | solution.py:39
  46.1 8.9 %spatial_heads.5 = bf16[320,5120]{1,0:T(8,128)(2,1)S(1)} custom-call(s32[160]{0:T(256)S(1)} %get-tuple-element.537.meta, bf16[320,5120]{1,0:T(8,128)(2,1)S(1)} %copy-done.1, bf16[320,5120]{1,0:T(8,128)(2,1)} %refs_11_.5, bf16[320,5120]{1,0:T(8,128)(2,1)} %refs_12_.5, ...), custom_call_target="tpu_custom_call", output_to_operand_aliasing={{}: (16, {})} | custom-call | flops 1572864000 | bytes 7372800 | tf_op jit(solution)/shard_map/spatial_heads/pallas_call | solution.py:264
  55.1 0.0 collective-permute-done.53
  55.1 0.0 collective-permute-done.51
  55.1 30.7 %conditional.1 = (bf16[320,5120]{1,0:T(8,128)(2,1)S(1)}) conditional(s32[]{:T(128)} %bitcast, (s32[160]{0:T(256)S(1)}, bf16[10,160,128]{2,1,0:T(8,128)(2,1)S(1)}, bf16[10,160,128]{2,1,0:T(8,128)(2,1)S(1)}, bf16[10,2,160,128]{3,2,1,0:T(8,128)(2,1)}, bf16[5,2,160,128]{3,2,1,0:T(8,128)(2,1)S(1)}, ...), branch_computations={%region_0.0_spmd, %region_1.0_spmd, %region_2.0_spmd, %region_3.0_... | conditional | flops 419430400 | bytes 20480248 | solution.py:544
  55.1 0.7 collective-permute-start.19
  55.8 1.3 %collective-permute-start.20 = (bf16[5,2,160,128]{3,2,1,0:T(8,128)(2,1)S(1)}, bf16[5,2,160,128]{3,2,1,0:T(8,128)(2,1)S(1)}, u32[]{:S(2)}, u32[]{:S(2)}) collective-permute-start(bf16[5,2,160,128]{3,2,1,0:T(8,128)(2,1)S(1)} %get-tuple-element.399.rest_5_), channel_id=1, source_target_pairs={{4,0},{5,1},{6,2},{7,3},{8,12},{9,13},{10,14},{11,15},{20,16},{21,... | collective-permute-start | bytes 1228808 | tf_op jit(solution)/shard_map/cond/branch_3_fun/ppermute | solution.py:39
  57.1 1.7 %temporal_heads.25 = (bf16[320,5120]{1,0:T(8,128)(2,1)S(1)}, bf16[1,160,128]{2,1,0:T(8,128)(2,1)S(1)}) custom-call(s32[160]{0:T(256)S(1)} %get-tuple-element.407.meta, bf16[10,160,128]{2,1,0:T(8,128)(2,1)S(1)} %get-tuple-element.406.query_own, bf16[10,160,128]{2,1,0:T(8,128)(2,1)S(1)} %get-tuple-element.387.query_far, ...), custom_call_target="tpu_custom_call", output_to_operand_aliasing={{0}: (9, {})} | custom-call | flops 41943040 | bytes 819200 | tf_op jit(solution)/shard_map/cond/branch_3_fun/temporal_heads/pallas_call | solution.py:431
  58.8 1.6 %pack_items.8 = (bf16[4,2,160,128]{3,2,1,0:T(8,128)(2,1)S(1)}, bf16[4,2,160,128]{3,2,1,0:T(8,128)(2,1)S(1)}) custom-call(s32[160]{0:T(256)S(1)} %get-tuple-element.407.meta, bf16[10,2,160,128]{3,2,1,0:T(8,128)(2,1)S(1)} %get-tuple-element.408.own_a, bf16[5,2,160,128]{3,2,1,0:T(8,128)(2,1)S(1)} %get-tuple-element.409.low_a, ...), custom_call_target="tpu_custom_call" | custom-call | tf_op jit(solution)/shard_map/cond/branch_3_fun/pack_items/pallas_call | solution.py:321
  60.4 1.3 %collective-permute-start.22 = (bf16[4,2,160,128]{3,2,1,0:T(8,128)(2,1)S(1)}, bf16[4,2,160,128]{3,2,1,0:T(8,128)(2,1)S(1)}, u32[]{:S(2)}, u32[]{:S(2)}) collective-permute-start(bf16[4,2,160,128]{3,2,1,0:T(8,128)(2,1)S(1)} %get-tuple-element.412), channel_id=1, source_target_pairs={{4,0},{5,1},{6,2},{7,3},{8,12},{9,13},{10,14},{11,15},{20,16},{21,... | collective-permute-start | bytes 983048 | tf_op jit(solution)/shard_map/cond/branch_3_fun/ppermute | solution.py:39
  61.7 0.7 collective-permute-start.23
  62.4 1.4 %collective-permute-start.18 = (bf16[1,160,128]{2,1,0:T(8,128)(2,1)S(1)}, bf16[1,160,128]{2,1,0:T(8,128)(2,1)S(1)}, u32[]{:S(2)}, u32[]{:S(2)}) collective-permute-start(bf16[1,160,128]{2,1,0:T(8,128)(2,1)S(1)} %get-tuple-element.395), channel_id=1, source_target_pairs={{0,2},{1,3},{2,0},{3,1},{4,6},{5,7},{6,4},{7,5},{8,10},{9,11},{10,... | collective-permute-start | bytes 122888 | tf_op jit(solution)/shard_map/cond/branch_3_fun/ppermute | solution.py:27
  63.8 7.2 %collective-permute-done.20.rest_9_ = bf16[5,2,160,128]{3,2,1,0:T(8,128)(2,1)S(1)} collective-permute-done((bf16[5,2,160,128]{3,2,1,0:T(8,128)(2,1)S(1)}, bf16[5,2,160,128]{3,2,1,0:T(8,128)(2,1)S(1)}, u32[]{:S(2)}, u32[]{:S(2)}) %collective-permute-start.20) | collective-permute-done | bytes 409632 | tf_op jit(solution)/shard_map/cond/branch_3_fun/ppermute | solution.py:39
  71.0 3.5 %temporal_heads.26 = (bf16[5,160,128]{2,1,0:T(8,128)(2,1)S(1)}, bf16[5,160,128]{2,1,0:T(8,128)(2,1)S(1)}) custom-call(s32[160]{0:T(256)S(1)} %get-tuple-element.407.meta, bf16[10,160,128]{2,1,0:T(8,128)(2,1)S(1)} %get-tuple-element.406.query_own, bf16[10,160,128]{2,1,0:T(8,128)(2,1)S(1)} %get-tuple-element.387.query_far, ...), custom_call_target="tpu_custom_call" | custom-call | flops 209715200 | bytes 4096000 | tf_op jit(solution)/shard_map/cond/branch_3_fun/temporal_heads/pallas_call | solution.py:431
  74.5 1.6 %collective-permute-start.21 = (bf16[5,160,128]{2,1,0:T(8,128)(2,1)S(1)}, bf16[5,160,128]{2,1,0:T(8,128)(2,1)S(1)}, u32[]{:S(2)}, u32[]{:S(2)}) collective-permute-start(bf16[5,160,128]{2,1,0:T(8,128)(2,1)S(1)} %get-tuple-element.405), channel_id=1, source_target_pairs={{0,2},{1,3},{2,0},{3,1},{4,6},{5,7},{6,4},{7,5},{8,10},{9,11},{10,... | collective-permute-start | bytes 614408 | tf_op jit(solution)/shard_map/cond/branch_3_fun/ppermute | solution.py:27
  76.1 0.0 collective-permute-done.18.refs_0_
  76.1 0.0 collective-permute-done.22.rest_6_
  76.1 0.0 collective-permute-done.23.rest_7_
  76.1 3.0 %temporal_heads.27 = (bf16[4,160,128]{2,1,0:T(8,128)(2,1)S(1)}, bf16[4,160,128]{2,1,0:T(8,128)(2,1)S(1)}) custom-call(s32[160]{0:T(256)S(1)} %get-tuple-element.407.meta, bf16[10,160,128]{2,1,0:T(8,128)(2,1)S(1)} %get-tuple-element.406.query_own, bf16[10,160,128]{2,1,0:T(8,128)(2,1)S(1)} %get-tuple-element.387.query_far, ...), custom_call_target="tpu_custom_call" | custom-call | flops 167772160 | bytes 3276800 | tf_op jit(solution)/shard_map/cond/branch_3_fun/temporal_heads/pallas_call | solution.py:431
  79.2 0.6 collective-permute-start.24
  79.8 4.8 %collective-permute-done.24.refs_4_ = bf16[4,160,128]{2,1,0:T(8,128)(2,1)S(1)} collective-permute-done((bf16[4,160,128]{2,1,0:T(8,128)(2,1)S(1)}, bf16[4,160,128]{2,1,0:T(8,128)(2,1)S(1)}, u32[]{:S(2)}, u32[]{:S(2)}) %collective-permute-start.24) | collective-permute-done | bytes 163872 | tf_op jit(solution)/shard_map/cond/branch_3_fun/ppermute | solution.py:27
  84.6 0.8 finish.10
  85.8 0.0 copy-start.2
  85.8 1.7 %copy-done.2 = bf16[320,5120]{1,0:T(8,128)(2,1)} copy-done((bf16[320,5120]{1,0:T(8,128)(2,1)}, bf16[320,5120]{1,0:T(8,128)(2,1)S(1)}, u32[]{:S(2)}) %copy-start.2) | copy-done | bytes 3276824
  (14 shorter events, 0.1 us)
Async XLA Ops:
  0.0 10.2 %copy-start = (bf16[320,5120]{1,0:T(8,128)(2,1)S(1)}, bf16[320,5120]{1,0:T(8,128)(2,1)}, u32[]{:S(2)}) copy-start(bf16[320,5120]{1,0:T(8,128)(2,1)} %refs_11_.5) | copy-start | bytes 9830404
  0.0 13.7 %collective-permute-start.47 = (bf16[320,5120]{1,0:T(8,128)(2,1)}, bf16[320,5120]{1,0:T(8,128)(2,1)}, u32[]{:S(2)}, u32[]{:S(2)}) collective-permute-start(bf16[320,5120]{1,0:T(8,128)(2,1)} %refs_11_.5), channel_id=1, source_target_pairs={{0,1},{1,0},{2,3},{3,2},{4,5},{5,4},{6,7},{7,6},{8,9},{9,8},{10,11... | collective-permute-start | bytes 9830408 | tf_op jit(solution)/shard_map/ppermute | solution.py:27
  0.5 13.7 %collective-permute-start.48 = (bf16[320,5120]{1,0:T(8,128)(2,1)}, bf16[320,5120]{1,0:T(8,128)(2,1)}, u32[]{:S(2)}, u32[]{:S(2)}) collective-permute-start(bf16[320,5120]{1,0:T(8,128)(2,1)} %refs_12_.5), channel_id=1, source_target_pairs={{0,1},{1,0},{2,3},{3,2},{4,5},{5,4},{6,7},{7,6},{8,9},{9,8},{10,11... | collective-permute-start | bytes 9830408 | tf_op jit(solution)/shard_map/ppermute | solution.py:27
  3.7 28.2 %collective-permute-start.44 = (bf16[10,2,160,128]{3,2,1,0:T(8,128)(2,1)}, bf16[10,2,160,128]{3,2,1,0:T(8,128)(2,1)S(1)}, u32[]{:S(2)}, u32[]{:S(2)}) collective-permute-start(bf16[10,2,160,128]{3,2,1,0:T(8,128)(2,1)} %get-tuple-element.533), channel_id=1, source_target_pairs={{4,8},{5,9},{6,10},{7,11},{8,4},{9,5},{10,6},{11,7},{20,24},{21,25... | collective-permute-start | bytes 2457608 | tf_op jit(solution)/shard_map/ppermute | solution.py:39
  4.4 27.4 %collective-permute-start.43 = (bf16[10,2,160,128]{3,2,1,0:T(8,128)(2,1)}, bf16[10,2,160,128]{3,2,1,0:T(8,128)(2,1)S(1)}, u32[]{:S(2)}, u32[]{:S(2)}) collective-permute-start(bf16[10,2,160,128]{3,2,1,0:T(8,128)(2,1)} %get-tuple-element.533), channel_id=1, source_target_pairs={{0,4},{1,5},{2,6},{3,7},{4,0},{5,1},{6,2},{7,3},{8,12},{9,13},{10,... | collective-permute-start | bytes 2457608 | tf_op jit(solution)/shard_map/ppermute | solution.py:39
  10.2 4.0 %copy-start.1 = (bf16[320,5120]{1,0:T(8,128)(2,1)S(1)}, bf16[320,5120]{1,0:T(8,128)(2,1)}, u32[]{:S(2)}) copy-start(bf16[320,5120]{1,0:T(8,128)(2,1)} %refs_10_.5) | copy-start | bytes 9830404
  12.1 12.5 %collective-permute-start.46 = (bf16[5,2,160,128]{3,2,1,0:T(8,128)(2,1)S(1)}, bf16[5,2,160,128]{3,2,1,0:T(8,128)(2,1)S(1)}, u32[]{:S(2)}, u32[]{:S(2)}) collective-permute-start(bf16[5,2,160,128]{3,2,1,0:T(8,128)(2,1)S(1)} %get-tuple-element.536), channel_id=1, source_target_pairs={{0,2},{1,3},{2,0},{3,1},{4,6},{5,7},{6,4},{7,5},{8,10},{9,11},{10,... | collective-permute-start | bytes 1228808 | tf_op jit(solution)/shard_map/ppermute | solution.py:27
  13.7 18.1 %collective-permute-start.45 = (bf16[5,2,160,128]{3,2,1,0:T(8,128)(2,1)S(1)}, bf16[5,2,160,128]{3,2,1,0:T(8,128)(2,1)S(1)}, u32[]{:S(2)}, u32[]{:S(2)}) collective-permute-start(bf16[5,2,160,128]{3,2,1,0:T(8,128)(2,1)S(1)} %get-tuple-element.535), channel_id=1, source_target_pairs={{0,2},{1,3},{2,0},{3,1},{4,6},{5,7},{6,4},{7,5},{8,10},{9,11},{10,... | collective-permute-start | bytes 1228808 | tf_op jit(solution)/shard_map/ppermute | solution.py:27
  24.6 12.5 %collective-permute-start.50 = (bf16[5,2,160,128]{3,2,1,0:T(8,128)(2,1)S(1)}, bf16[5,2,160,128]{3,2,1,0:T(8,128)(2,1)S(1)}, u32[]{:S(2)}, u32[]{:S(2)}) collective-permute-start(bf16[5,2,160,128]{3,2,1,0:T(8,128)(2,1)S(1)} %collective-permute-done.46), channel_id=1, source_target_pairs={{4,8},{5,9},{6,10},{7,11},{8,4},{9,5},{10,6},{11,7},{20,24},{21,25... | collective-permute-start | bytes 1228808 | tf_op jit(solution)/shard_map/ppermute | solution.py:39
  25.2 13.0 %collective-permute-start.49 = (bf16[5,2,160,128]{3,2,1,0:T(8,128)(2,1)S(1)}, bf16[5,2,160,128]{3,2,1,0:T(8,128)(2,1)S(1)}, u32[]{:S(2)}, u32[]{:S(2)}) collective-permute-start(bf16[5,2,160,128]{3,2,1,0:T(8,128)(2,1)S(1)} %collective-permute-done.46), channel_id=1, source_target_pairs={{0,4},{1,5},{2,6},{3,7},{4,0},{5,1},{6,2},{7,3},{8,12},{9,13},{10,... | collective-permute-start | bytes 1228808 | tf_op jit(solution)/shard_map/ppermute | solution.py:39
  31.8 3.7 %collective-permute-start.56 = (s32[1]{0:T(128)}, s32[1]{0:T(128)}, u32[]{:S(2)}, u32[]{:S(2)}) collective-permute-start(s32[1]{0:T(128)} %get-tuple-element.551), channel_id=1, source_target_pairs={{0,16},{16,0},{1,17},{17,1},{2,18},{18,2},{3,19},{19,3},{4,20},{20... | collective-permute-start | bytes 20 | tf_op jit(solution)/shard_map/ppermute | solution.py:47
  33.4 21.7 %collective-permute-start.54 = (bf16[5,2,160,128]{3,2,1,0:T(8,128)(2,1)S(1)}, bf16[5,2,160,128]{3,2,1,0:T(8,128)(2,1)S(1)}, u32[]{:S(2)}, u32[]{:S(2)}) collective-permute-start(bf16[5,2,160,128]{3,2,1,0:T(8,128)(2,1)S(1)} %slice.7), channel_id=1, source_target_pairs={{4,0},{5,1},{6,2},{7,3},{8,12},{9,13},{10,14},{11,15},{20,16},{21,... | collective-permute-start | bytes 1228808 | tf_op jit(solution)/shard_map/ppermute | solution.py:39
  34.7 20.4 %collective-permute-start.53 = (bf16[5,2,160,128]{3,2,1,0:T(8,128)(2,1)S(1)}, bf16[5,2,160,128]{3,2,1,0:T(8,128)(2,1)S(1)}, u32[]{:S(2)}, u32[]{:S(2)}) collective-permute-start(bf16[5,2,160,128]{3,2,1,0:T(8,128)(2,1)S(1)} %slice.6), channel_id=1, source_target_pairs={{4,8},{5,9},{6,10},{7,11},{8,4},{9,5},{10,6},{11,7},{20,24},{21,25... | collective-permute-start | bytes 1228808 | tf_op jit(solution)/shard_map/ppermute | solution.py:39
  35.5 19.5 %collective-permute-start.55 = (bf16[10,160,128]{2,1,0:T(8,128)(2,1)S(1)}, bf16[10,160,128]{2,1,0:T(8,128)(2,1)S(1)}, u32[]{:S(2)}, u32[]{:S(2)}) collective-permute-start(bf16[10,160,128]{2,1,0:T(8,128)(2,1)S(1)} %get-tuple-element.550), channel_id=1, source_target_pairs={{0,2},{1,3},{2,0},{3,1},{4,6},{5,7},{6,4},{7,5},{8,10},{9,11},{10,... | collective-permute-start | bytes 1228808 | tf_op jit(solution)/shard_map/ppermute | solution.py:27
  37.0 18.0 %collective-permute-start.52 = (bf16[5,2,160,128]{3,2,1,0:T(8,128)(2,1)S(1)}, bf16[5,2,160,128]{3,2,1,0:T(8,128)(2,1)S(1)}, u32[]{:S(2)}, u32[]{:S(2)}) collective-permute-start(bf16[5,2,160,128]{3,2,1,0:T(8,128)(2,1)S(1)} %collective-permute-done.45), channel_id=1, source_target_pairs={{4,8},{5,9},{6,10},{7,11},{8,4},{9,5},{10,6},{11,7},{20,24},{21,25... | collective-permute-start | bytes 1228808 | tf_op jit(solution)/shard_map/ppermute | solution.py:39
  38.3 16.8 %collective-permute-start.51 = (bf16[5,2,160,128]{3,2,1,0:T(8,128)(2,1)S(1)}, bf16[5,2,160,128]{3,2,1,0:T(8,128)(2,1)S(1)}, u32[]{:S(2)}, u32[]{:S(2)}) collective-permute-start(bf16[5,2,160,128]{3,2,1,0:T(8,128)(2,1)S(1)} %collective-permute-done.45), channel_id=1, source_target_pairs={{0,4},{1,5},{2,6},{3,7},{4,0},{5,1},{6,2},{7,3},{8,12},{9,13},{10,... | collective-permute-start | bytes 1228808 | tf_op jit(solution)/shard_map/ppermute | solution.py:39
  55.1 8.7 %collective-permute-start.19 = (bf16[5,2,160,128]{3,2,1,0:T(8,128)(2,1)S(1)}, bf16[5,2,160,128]{3,2,1,0:T(8,128)(2,1)S(1)}, u32[]{:S(2)}, u32[]{:S(2)}) collective-permute-start(bf16[5,2,160,128]{3,2,1,0:T(8,128)(2,1)S(1)} %get-tuple-element.398.rest_3_), channel_id=1, source_target_pairs={{4,8},{5,9},{6,10},{7,11},{8,4},{9,5},{10,6},{11,7},{20,24},{21,25... | collective-permute-start | bytes 1228808 | tf_op jit(solution)/shard_map/cond/branch_3_fun/ppermute | solution.py:39
  55.8 15.2 %collective-permute-start.20 = (bf16[5,2,160,128]{3,2,1,0:T(8,128)(2,1)S(1)}, bf16[5,2,160,128]{3,2,1,0:T(8,128)(2,1)S(1)}, u32[]{:S(2)}, u32[]{:S(2)}) collective-permute-start(bf16[5,2,160,128]{3,2,1,0:T(8,128)(2,1)S(1)} %get-tuple-element.399.rest_5_), channel_id=1, source_target_pairs={{4,0},{5,1},{6,2},{7,3},{8,12},{9,13},{10,14},{11,15},{20,16},{21,... | collective-permute-start | bytes 1228808 | tf_op jit(solution)/shard_map/cond/branch_3_fun/ppermute | solution.py:39
  60.4 15.7 %collective-permute-start.22 = (bf16[4,2,160,128]{3,2,1,0:T(8,128)(2,1)S(1)}, bf16[4,2,160,128]{3,2,1,0:T(8,128)(2,1)S(1)}, u32[]{:S(2)}, u32[]{:S(2)}) collective-permute-start(bf16[4,2,160,128]{3,2,1,0:T(8,128)(2,1)S(1)} %get-tuple-element.412), channel_id=1, source_target_pairs={{4,0},{5,1},{6,2},{7,3},{8,12},{9,13},{10,14},{11,15},{20,16},{21,... | collective-permute-start | bytes 983048 | tf_op jit(solution)/shard_map/cond/branch_3_fun/ppermute | solution.py:39
  61.7 14.4 %collective-permute-start.23 = (bf16[4,2,160,128]{3,2,1,0:T(8,128)(2,1)S(1)}, bf16[4,2,160,128]{3,2,1,0:T(8,128)(2,1)S(1)}, u32[]{:S(2)}, u32[]{:S(2)}) collective-permute-start(bf16[4,2,160,128]{3,2,1,0:T(8,128)(2,1)S(1)} %get-tuple-element.413), channel_id=1, source_target_pairs={{4,8},{5,9},{6,10},{7,11},{8,4},{9,5},{10,6},{11,7},{20,24},{21,25... | collective-permute-start | bytes 983048 | tf_op jit(solution)/shard_map/cond/branch_3_fun/ppermute | solution.py:39
  62.4 13.7 %collective-permute-start.18 = (bf16[1,160,128]{2,1,0:T(8,128)(2,1)S(1)}, bf16[1,160,128]{2,1,0:T(8,128)(2,1)S(1)}, u32[]{:S(2)}, u32[]{:S(2)}) collective-permute-start(bf16[1,160,128]{2,1,0:T(8,128)(2,1)S(1)} %get-tuple-element.395), channel_id=1, source_target_pairs={{0,2},{1,3},{2,0},{3,1},{4,6},{5,7},{6,4},{7,5},{8,10},{9,11},{10,... | collective-permute-start | bytes 122888 | tf_op jit(solution)/shard_map/cond/branch_3_fun/ppermute | solution.py:27
  74.5 10.0 %collective-permute-start.21 = (bf16[5,160,128]{2,1,0:T(8,128)(2,1)S(1)}, bf16[5,160,128]{2,1,0:T(8,128)(2,1)S(1)}, u32[]{:S(2)}, u32[]{:S(2)}) collective-permute-start(bf16[5,160,128]{2,1,0:T(8,128)(2,1)S(1)} %get-tuple-element.405), channel_id=1, source_target_pairs={{0,2},{1,3},{2,0},{3,1},{4,6},{5,7},{6,4},{7,5},{8,10},{9,11},{10,... | collective-permute-start | bytes 614408 | tf_op jit(solution)/shard_map/cond/branch_3_fun/ppermute | solution.py:27
  79.2 5.4 %collective-permute-start.24 = (bf16[4,160,128]{2,1,0:T(8,128)(2,1)S(1)}, bf16[4,160,128]{2,1,0:T(8,128)(2,1)S(1)}, u32[]{:S(2)}, u32[]{:S(2)}) collective-permute-start(bf16[4,160,128]{2,1,0:T(8,128)(2,1)S(1)} %get-tuple-element.415), channel_id=1, source_target_pairs={{0,2},{1,3},{2,0},{3,1},{4,6},{5,7},{6,4},{7,5},{8,10},{9,11},{10,... | collective-permute-start | bytes 491528 | tf_op jit(solution)/shard_map/cond/branch_3_fun/ppermute | solution.py:27
  85.8 1.7 %copy-start.2 = (bf16[320,5120]{1,0:T(8,128)(2,1)}, bf16[320,5120]{1,0:T(8,128)(2,1)S(1)}, u32[]{:S(2)}) copy-start(bf16[320,5120]{1,0:T(8,128)(2,1)S(1)} %get-tuple-element.649) | copy-start | bytes 9830404
